TPU v7x, 32 devices: a whole 2x2x4 slice. The times are simulated.
32 devices in a mesh: dp: 8 (over z, x), row: 2 (over y), col: 2 (over core).
Axes of the slice: x: 2, y: 2, z: 4, core: 2. Of those that a mesh axis runs over, the one named last changes fastest.
Arguments:
- block_in: bfloat16 [3072, 768], P('dp'), may hold values from -6 to 6
- lengths: int32 [4], replicated, may hold values from 1 to 1536, as said below
- attend_in: bfloat16 [768, 2304], P('col', 'row'), may hold values from -0.21875 to 0.21875
- query_bias: float32 [768], replicated, may hold values from -1.75 to 1.75
- value_bias: float32 [768], replicated, may hold values from -1.75 to 1.75
- attend_out: bfloat16 [768, 768], P('col', 'row'), may hold values from -0.875 to 0.875
- out_bias: float32 [768], replicated, may hold values from -1.75 to 1.75
- gain_first: float32 [768], replicated, may hold values from 0.5 to 1.5
- shift_first: float32 [768], replicated, may hold values from -1.75 to 1.75
- gain_second: float32 [768], replicated, may hold values from 0.5 to 1.5
- shift_second: float32 [768], replicated, may hold values from -1.75 to 1.75
- up_weight: bfloat16 [768, 3072], P('col', 'row'), may hold values from -0.21875 to 0.21875
- up_bias: float32 [3072], replicated, may hold values from -1.75 to 1.75
- down_weight: bfloat16 [3072, 768], P('col', 'row'), may hold values from -0.109375 to 0.109375
- down_bias: float32 [768], replicated, may hold values from -1.75 to 1.75
- grad_out: bfloat16 [3072, 768], P('dp', ('row', 'col')), may hold values from -6 to 6
Outputs:
- block_out: float32 [3072, 768], P('dp', ('row', 'col'))
- grad_in: bfloat16 [3072, 768], P('dp', ('row', 'col'))
- grad_attend_in: float32 [768, 2304], P('col', 'row')
- grad_query_bias: float32 [768], replicated
- grad_value_bias: float32 [768], replicated
- grad_attend_out: float32 [768, 768], P('col', 'row')
- grad_out_bias: float32 [768], replicated
- grad_gain_first: float32 [768], replicated
- grad_shift_first: float32 [768], replicated
- grad_gain_second: float32 [768], replicated
- grad_shift_second: float32 [768], replicated
- grad_up_weight: float32 [768, 3072], P('col', 'row')
- grad_up_bias: float32 [3072], replicated
- grad_down_weight: float32 [3072, 768], P('col', 'row')
- grad_down_bias: float32 [768], replicated
Inputs may be any that keep to these rules, and one draw needn't show every extreme that they name: The lengths sum to 3072; exactly one sequence, neither the first nor the last, has 1536 tokens; no sequence ends at a multiple of 384 except the last.
All inputs are finite; a program needn't handle non-finite values.
Results may differ from a plain program's by a relative error of at most 0.025.
Values may be sent and summed in bfloat16 or wider, within the bound.
A program may use at most 128 MiB of HBM per device.

v0:
```python
import jax
import jax.numpy as jnp
from jax import lax
from jax.sharding import PartitionSpec as P

H = 12
LONGEST = 4096
HMAX = 4


EPSILON = 1e-05
FLOOR = -1e30


def from_behind(array, axis, by):
    length = lax.axis_size(axis)
    pairs = [(i, i + by) for i in range(length) if 0 <= i + by < length]
    return lax.ppermute(array, axis, pairs)


def shifted(block, axis, distance):
    devices = range(lax.axis_size(axis))
    route = [((i - distance) % len(devices), i) for i in devices]
    return lax.ppermute(block, axis, route)


def layer_norm(stream, norm_gain, norm_shift):
    center = jnp.mean(stream, axis=-1, keepdims=True)
    centred = stream - center
    spread = jnp.mean(centred * centred, axis=-1, keepdims=True)
    return centred * lax.rsqrt(spread + EPSILON) * norm_gain + norm_shift


def smooth_gate(values):
    return jax.nn.gelu(values, approximate=True)


def slice_cols(source, block_index, extent):
    return lax.dynamic_slice_in_dim(source, block_index * extent, extent, source.ndim - 1)


def forward_part(full_rows, weight_block, col_index):
    inputs = slice_cols(full_rows, col_index, weight_block.shape[0])
    partial_value = jnp.dot(inputs, weight_block, preferred_element_type=jnp.float32)
    return lax.psum_scatter(
        partial_value.astype(jnp.bfloat16), "col", scatter_dimension=1, tiled=True
    ).astype(jnp.float32)


def spread_low(share_rows):
    return lax.all_gather(share_rows, ("row", "col"), axis=1, tiled=True)


def backward_part(grad_full, weight_block, row_index):
    inputs = slice_cols(grad_full, row_index, weight_block.shape[1])
    partial_value = lax.dot_general(
        inputs, weight_block, (((1,), (1,)), ((), ())), preferred_element_type=jnp.float32
    )
    share_rows = lax.psum_scatter(
        partial_value.astype(jnp.bfloat16), "row", scatter_dimension=1, tiled=True
    ).astype(jnp.float32)
    pieces = lax.all_gather(
        share_rows.astype(jnp.bfloat16), ("row", "col"), axis=1, tiled=True
    ).astype(share_rows.dtype)
    row_count = lax.axis_size("row")
    col_count = lax.axis_size("col")
    token_rows = pieces.shape[0]
    share_width = share_rows.shape[1]
    pieces = pieces.reshape(token_rows, row_count, col_count, share_width).swapaxes(1, 2)
    return pieces.reshape(token_rows, row_count * col_count * share_width)


def weight_grad(inputs, grads, weight_block, row_index, col_index):
    left_rows = slice_cols(inputs, col_index, weight_block.shape[0])
    right_rows = slice_cols(grads, row_index, weight_block.shape[1])
    return lax.dot_general(
        left_rows, right_rows, (((0,), (0,)), ((), ())), preferred_element_type=jnp.float32
    )


def sequence_ids(positions, lengths):
    bounds = jnp.cumsum(lengths)
    return jnp.sum((bounds[None, :] <= positions[:, None]).astype(jnp.int32), axis=1)


def key_mask(q_pos, q_seq, source, lengths):
    token_rows = q_pos.shape[0]
    k_pos = source * token_rows + jnp.arange(token_rows, dtype=jnp.int32)
    k_seq = sequence_ids(k_pos, lengths)
    allowed = (q_seq[:, None] == k_seq[None, :]) & (k_pos[None, :] <= q_pos[:, None])
    return allowed[:, None, :]


def scores_of(queries, keys):
    score_scale = queries.shape[-1] ** (-0.5)
    return (
        jnp.einsum("qsd,ksd->qsk", queries, keys, preferred_element_type=jnp.float32) * score_scale
    )


def query_places(token_rows, lengths):
    own_group = lax.axis_index("dp")
    q_pos = own_group * token_rows + jnp.arange(token_rows, dtype=jnp.int32)
    return (own_group, q_pos, sequence_ids(q_pos, lengths))


def attend(queries, keys, values, lengths, visits):
    token_rows, slot_count, head_size = queries.shape
    group_count = lax.axis_size("dp")
    own_group, q_pos, q_seq = query_places(token_rows, lengths)

    def visit(state, key_pair, source):
        running_max, running_sum, running_out = state
        allowed = key_mask(q_pos, q_seq, source, lengths)
        scores = jnp.where(allowed, scores_of(queries, key_pair[0]), FLOOR)
        new_max = jnp.maximum(running_max, jnp.max(scores, axis=2))
        weights = jnp.where(allowed, jnp.exp(scores - new_max[:, :, None]), 0.0)
        factor = jnp.exp(running_max - new_max)
        running_sum = running_sum * factor + jnp.sum(weights, axis=2)
        update = jnp.einsum(
            "qsk,ksd->qsd",
            weights.astype(jnp.bfloat16),
            key_pair[1],
            preferred_element_type=jnp.float32,
        )
        running_out = running_out * factor[:, :, None] + update
        return (new_max, running_sum, running_out)

    initial = (
        jnp.full((token_rows, slot_count), FLOOR, jnp.float32),
        jnp.zeros((token_rows, slot_count), jnp.float32),
        jnp.zeros((token_rows, slot_count, head_size), jnp.float32),
    )
    key_pair = jnp.stack([keys, values])
    state = visit(initial, key_pair, own_group)

    def advance(carry, visit_turn):
        key_pair, state = carry
        key_pair = from_behind(key_pair, "dp", 1)
        state = visit(state, key_pair, (own_group - visit_turn) % group_count)
        return ((key_pair, state), key_pair)

    turns = jnp.arange(1, visits + 1, dtype=jnp.int32)
    (key_pair, state), kept_pairs = lax.scan(advance, (key_pair, state), turns)
    running_max, running_sum, running_out = state
    return (running_out / running_sum[:, :, None], running_max + jnp.log(running_sum), kept_pairs)


def carry_grads(pair_grads):
    return shifted(pair_grads.astype(jnp.bfloat16), "dp", 1).astype(pair_grads.dtype)


def attend_back(queries, keys, values, d_out, exact, log_total, lengths, visits):
    token_rows = queries.shape[0]
    group_count = lax.axis_size("dp")
    own_group, q_pos, q_seq = query_places(token_rows, lengths)
    delta = jnp.sum(d_out.astype(jnp.float32) * exact, axis=2)
    score_scale = queries.shape[-1] ** (-0.5)

    def visit(key_pair, source):
        allowed = key_mask(q_pos, q_seq, source, lengths)
        weights = jnp.where(
            allowed, jnp.exp(scores_of(queries, key_pair[0]) - log_total[:, :, None]), 0.0
        )
        d_values = jnp.einsum(
            "qsk,qsd->ksd", weights.astype(jnp.bfloat16), d_out, preferred_element_type=jnp.float32
        )
        d_weights = jnp.einsum(
            "qsd,ksd->qsk", d_out, key_pair[1], preferred_element_type=jnp.float32
        )
        d_scores = (weights * (d_weights - delta[:, :, None]) * score_scale).astype(jnp.bfloat16)
        d_query = jnp.einsum(
            "qsk,ksd->qsd", d_scores, key_pair[0], preferred_element_type=jnp.float32
        )
        d_keys = jnp.einsum("qsk,qsd->ksd", d_scores, queries, preferred_element_type=jnp.float32)
        return (d_query, jnp.stack([d_keys, d_values]))

    d_query, pair_grads = visit(jnp.stack([keys, values]), own_group)
    turns = jnp.arange(1, visits + 1, dtype=jnp.int32)

    def advance(carry, visit_turn):
        key_pair, pair_grads, d_query = carry
        key_pair = from_behind(key_pair, "dp", 1)
        pair_grads = carry_grads(pair_grads)
        part_query, part_pair = visit(key_pair, (own_group - visit_turn) % group_count)
        return ((key_pair, pair_grads + part_pair, d_query + part_query), None)

    (key_pair, pair_grads, d_query), unused = lax.scan(
        advance, (jnp.stack([keys, values]), pair_grads, d_query), turns
    )
    pair_grads = shifted(pair_grads.astype(jnp.bfloat16), "dp", -visits).astype(pair_grads.dtype)
    return (d_query, pair_grads[0], pair_grads[1])


def shards(
    block_in,
    lengths,
    attend_in,
    query_bias,
    value_bias,
    attend_out,
    out_bias,
    gain_first,
    shift_first,
    gain_second,
    shift_second,
    up_weight,
    up_bias,
    down_weight,
    down_bias,
    grad_out,
):
    row_index = lax.axis_index("row")
    col_index = lax.axis_index("col")
    col_count = lax.axis_size("col")
    grid_size = lax.axis_size("row") * col_count
    grid_place = row_index * col_count + col_index
    token_rows, model = block_in.shape
    heads = H
    head_size = model // heads
    group_count = lax.axis_size("dp")
    longest_here = min(LONGEST, token_rows * group_count // 2)
    reach_groups = (longest_here - 2 + token_rows) // token_rows
    visits = min(reach_groups, group_count - 1)
    places = jnp.arange(heads, dtype=jnp.int32)
    head_owner = jnp.where(places < HMAX, 0, 1 + (places - HMAX) % (grid_size - 1))
    owned = (head_owner[:, None] == jnp.arange(grid_size, dtype=jnp.int32)[None, :]).astype(
        jnp.int32
    )
    ranking = jnp.sum((jnp.cumsum(owned, axis=0) - 1) * owned, axis=1)
    picks = (owned.T[:, None, :] == 1) & (
        ranking[None, None, :] == jnp.arange(HMAX, dtype=jnp.int32)[None, :, None]
    )
    picks = picks.astype(jnp.bfloat16)
    mine = lax.dynamic_index_in_dim(picks, grid_place, 0, keepdims=False)
    stream = block_in.astype(jnp.float32)
    h_first = layer_norm(stream, gain_first, shift_first).astype(jnp.bfloat16)
    qkv_bias = jnp.concatenate([query_bias, jnp.zeros_like(query_bias), value_bias])
    qkv_share = forward_part(h_first, attend_in, col_index)
    qkv_share = (qkv_share + slice_cols(qkv_bias, grid_place, qkv_share.shape[1])).astype(
        jnp.bfloat16
    )
    qkv_full = spread_low(qkv_share).reshape(token_rows, 3, heads, head_size)
    slot_qkv = jnp.einsum(
        "tjhd,sh->tjsd", qkv_full, mine, preferred_element_type=jnp.float32
    ).astype(jnp.bfloat16)
    queries = slot_qkv[:, 0]
    keys = slot_qkv[:, 1]
    values = slot_qkv[:, 2]
    exact, log_total, kept_pairs = attend(queries, keys, values, lengths, visits)
    slot_out = exact.astype(jnp.bfloat16).reshape(1, token_rows, HMAX * head_size)
    all_out = lax.all_gather(slot_out, ("row", "col"), axis=0, tiled=True).reshape(
        grid_size, token_rows, HMAX, head_size
    )
    mixed = jnp.einsum("gtsd,gsh->thd", all_out, picks, preferred_element_type=jnp.float32)
    mixed = mixed.astype(jnp.bfloat16).reshape(token_rows, model)
    branch_share = forward_part(mixed, attend_out, col_index)
    branch_share = branch_share + slice_cols(out_bias, grid_place, branch_share.shape[1])
    r_first = stream + lax.all_gather(
        branch_share.astype(jnp.bfloat16), ("row", "col"), axis=1, tiled=True
    ).astype(branch_share.dtype)
    h_second = layer_norm(r_first, gain_second, shift_second).astype(jnp.bfloat16)
    gate_share = forward_part(h_second, up_weight, col_index)
    gate_share = gate_share + slice_cols(up_bias, grid_place, gate_share.shape[1])
    hidden = spread_low(smooth_gate(gate_share).astype(jnp.bfloat16))
    down_share = forward_part(hidden, down_weight, col_index)
    share_width = down_share.shape[1]
    block_out = slice_cols(r_first, grid_place, share_width) + (
        down_share + slice_cols(down_bias, grid_place, share_width)
    )
    grad_full = spread_low(grad_out)
    g_down_weight = weight_grad(hidden, grad_full, down_weight, row_index, col_index)
    g_down_bias = jnp.sum(grad_full, axis=0, dtype=jnp.float32)
    d_hidden = backward_part(grad_full, down_weight, row_index)
    gate_pull = jax.vjp(smooth_gate, gate_share)[1]
    d_gate_share = gate_pull(slice_cols(d_hidden, grid_place, gate_share.shape[1]))[0].astype(
        jnp.bfloat16
    )
    d_gate = spread_low(d_gate_share)
    g_up_weight = weight_grad(h_second, d_gate, up_weight, row_index, col_index)
    g_up_bias = jnp.sum(d_gate, axis=0, dtype=jnp.float32)
    d_h_second = backward_part(d_gate, up_weight, row_index)
    second_pull = jax.vjp(layer_norm, r_first, gain_second, shift_second)[1]
    d_norm_second, g_gain_second, g_shift_second = second_pull(d_h_second)
    d_r_first = grad_full.astype(jnp.float32) + d_norm_second
    d_branch = d_r_first.astype(jnp.bfloat16)
    g_attend_out = weight_grad(mixed, d_branch, attend_out, row_index, col_index)
    g_out_bias = jnp.sum(d_branch, axis=0, dtype=jnp.float32)
    d_mixed = (
        backward_part(d_branch, attend_out, row_index)
        .astype(jnp.bfloat16)
        .reshape(token_rows, heads, head_size)
    )
    d_slots = jnp.einsum("thd,sh->tsd", d_mixed, mine, preferred_element_type=jnp.float32).astype(
        jnp.bfloat16
    )
    d_query, d_keys, d_values = attend_back(
        queries, keys, values, d_slots, exact, log_total, lengths, visits
    )
    d_slot_qkv = jnp.stack([d_query, d_keys, d_values], axis=1).astype(jnp.bfloat16)
    d_slot_qkv = d_slot_qkv.reshape(1, token_rows, 3 * HMAX * head_size)
    all_grads = lax.all_gather(d_slot_qkv, ("row", "col"), axis=0, tiled=True).reshape(
        grid_size, token_rows, 3, HMAX, head_size
    )
    d_qkv = jnp.einsum("gtjsd,gsh->tjhd", all_grads, picks, preferred_element_type=jnp.float32)
    d_qkv = d_qkv.astype(jnp.bfloat16).reshape(token_rows, 3 * model)
    g_attend_in = weight_grad(h_first, d_qkv, attend_in, row_index, col_index)
    column_sums = jnp.sum(d_qkv, axis=0, dtype=jnp.float32).reshape(3, model)
    g_query_bias = column_sums[0]
    g_value_bias = column_sums[2]
    d_h_first = backward_part(d_qkv, attend_in, row_index)
    first_pull = jax.vjp(layer_norm, stream, gain_first, shift_first)[1]
    d_norm_first, g_gain_first, g_shift_first = first_pull(d_h_first)
    grad_in = slice_cols(d_r_first + d_norm_first, grid_place, share_width).astype(jnp.bfloat16)
    summed = lax.psum(
        (
            g_down_weight,
            g_down_bias,
            g_up_weight,
            g_up_bias,
            g_gain_second,
            g_shift_second,
            g_attend_in,
            g_query_bias,
            g_value_bias,
            g_attend_out,
            g_out_bias,
            g_gain_first,
            g_shift_first,
        ),
        "dp",
    )
    g_down_weight, g_down_bias, g_up_weight, g_up_bias, g_gain_second, g_shift_second = summed[:6]
    (
        g_attend_in,
        g_query_bias,
        g_value_bias,
        g_attend_out,
        g_out_bias,
        g_gain_first,
        g_shift_first,
    ) = summed[6:]
    return (
        block_out,
        grad_in,
        g_attend_in,
        g_query_bias,
        g_value_bias,
        g_attend_out,
        g_out_bias,
        g_gain_first,
        g_shift_first,
        g_gain_second,
        g_shift_second,
        g_up_weight,
        g_up_bias,
        g_down_weight,
        g_down_bias,
    )


def solution(mesh):
    placed = (
        P("dp", None),
        P(),
        P("col", "row"),
        P(),
        P(),
        P("col", "row"),
        P(),
        P(),
        P(),
        P(),
        P(),
        P("col", "row"),
        P(),
        P("col", "row"),
        P(),
        P("dp", ("row", "col")),
    )
    return jax.shard_map(
        shards,
        mesh=mesh,
        in_specs=placed,
        out_specs=(
            P("dp", ("row", "col")),
            P("dp", ("row", "col")),
            P("col", "row"),
            P(),
            P(),
            P("col", "row"),
            P(),
            P(),
            P(),
            P(),
            P(),
            P("col", "row"),
            P(),
            P("col", "row"),
            P(),
        ),
        check_vma=False,
    )
```

profile of v0, /device:TPU:0, one launch (start us, length us, event | category | flops | bytes accessed | tf_op | source)
XLA Modules:
  0.0 692.3 jit_solution(12551553367586902305)
XLA Ops:
  14.8 11.0 %reduce-scatter.9.cloned.1.call-done = bf16[384,576]{0,1:T(8,128)(2,1)} async-done(((bf16[384,1152]{0,1:T(8,128)(2,1)}), bf16[384,576]{0,1:T(8,128)(2,1)}) %reduce-scatter.9.cloned.1.call-update) | async-done | bytes 442384 | tf_op jit(solution)/shard_map/reduce_scatter | solution.py:45
  27.8 7.7 %all_gather.37 = bf16[384,768]{0,1:T(8,128)(2,1)S(1)} all-gather(bf16[384,192]{0,1:T(8,128)(2,1)S(1)} %copy-done.41), channel_id=1, replica_groups=mesh['dp'=8,'row'=2,'col'=2] {'row','col'}, dimensions={1}, use_global_device_ids=true | all-gather | bytes 737280 | tf_op jit(solution)/shard_map/all_gather | solution.py:51
  40.2 10.0 %all-gather.6.cloned.1.call-done = bf16[384,2304]{0,1:T(8,128)(2,1)} async-done(((bf16[384,576]{0,1:T(8,128)(2,1)}), bf16[384,2304]{0,1:T(8,128)(2,1)}) %all-gather.6.cloned.1.call-update) | async-done | bytes 1769488 | tf_op jit(solution)/shard_map/all_gather | solution.py:51
  57.3 59.6 %while.36 = (s32[]{:T(128)}, bf16[2,384,4,64]{1,3,2,0:T(8,128)(2,1)S(1)}, f32[384,4]{0,1:T(4,128)S(1)}, f32[384,4]{0,1:T(4,128)S(1)}, f32[384,4,64]{0,2,1:T(8,12...) while((s32[]{:T(128)}, ...), condition=%wide.region_13.14_spmd.clone, body=%wide.region_9.13_spmd.clone.sunk | while | flops 159309712 | bytes 14659998 | solution.py:144
  118.8 7.8 %all_gather.34 = bf16[4,384,256]{2,1,0:T(8,128)(2,1)S(1)} all-gather(bf16[1,384,256]{2,1,0:T(8,128)(2,1)} %copy.224), channel_id=1, replica_groups=mesh['dp'=8,'row'=2,'col'=2] {'row','col'}, dimensions={0}, use_global_device_ids=true | all-gather | bytes 983040 | tf_op jit(solution)/shard_map/all_gather | solution.py:252
  133.9 9.7 %reduce-scatter.11.cloned.1.call-done = bf16[384,192]{0,1:T(8,128)(2,1)} async-done(((bf16[384,384]{0,1:T(8,128)(2,1)}), bf16[384,192]{0,1:T(8,128)(2,1)}) %reduce-scatter.11.cloned.1.call-update) | async-done | bytes 147472 | tf_op jit(solution)/shard_map/reduce_scatter | solution.py:45
  144.6 10.8 %all_gather.35 = bf16[384,768]{0,1:T(8,128)(2,1)S(1)} all-gather(bf16[384,192]{0,1:T(8,128)(2,1)S(1)} %add_convert_fusion.1), channel_id=1, replica_groups=mesh['dp'=8,'row'=2,'col'=2] {'row','col'}, dimensions={1}, use_global_device_ids=true | all-gather | bytes 737280 | tf_op jit(solution)/shard_map/all_gather | solution.py:259
  172.3 6.9 %copy.299 = f32[384,2,2,768]{3,1,2,0:T(2,128)} copy(f32[384,2,2,768]{3,2,1,0:T(2,128)} %reshape.452) | data formatting | bytes 9437184 | tf_op jit(solution)/shard_map/reshape | solution.py:70
  179.3 7.0 %reshape.447 = f32[384,3072]{1,0:T(8,128)} reshape(f32[384,2,2,768]{3,2,1,0:T(2,128)} %bitcast.284) | data formatting | bytes 9437184 | tf_op jit(solution)/shard_map/reshape | solution.py:70
  189.7 24.1 %all-gather.12.cloned.1.call-done = bf16[384,3072]{1,0:T(8,128)(2,1)} async-done(((bf16[384,768]{1,0:T(8,128)(2,1)}), bf16[384,3072]{1,0:T(8,128)(2,1)}) %all-gather.12.cloned.1.call-update) | async-done | bytes 2359312 | tf_op jit(solution)/shard_map/all_gather | solution.py:51
  216.7 12.0 %reduce-scatter.19.cloned.1.call-done = bf16[384,192]{0,1:T(8,128)(2,1)} async-done(((bf16[384,384]{0,1:T(8,128)(2,1)}), bf16[384,192]{0,1:T(8,128)(2,1)}) %reduce-scatter.19.cloned.1.call-update) | async-done | bytes 147472 | tf_op jit(solution)/shard_map/reduce_scatter | solution.py:59
  228.7 7.3 %all_gather.40 = bf16[384,768]{0,1:T(8,128)(2,1)S(1)} all-gather(bf16[384,192]{0,1:T(8,128)(2,1)} %reduce-scatter.19.cloned.1.call-done), channel_id=1, replica_groups=mesh['dp'=8,'row'=2,'col'=2] {'row','col'}, dimensions={1}, use_global_device_ids=true | all-gather | bytes 737280 | tf_op jit(solution)/shard_map/all_gather | solution.py:62
  244.7 11.9 %reduce-scatter.21.cloned.1.call-done = bf16[384,192]{0,1:T(8,128)(2,1)} async-done(((bf16[384,384]{0,1:T(8,128)(2,1)}), bf16[384,192]{0,1:T(8,128)(2,1)}) %reduce-scatter.21.cloned.1.call-update) | async-done | bytes 147472 | tf_op jit(solution)/shard_map/reduce_scatter | solution.py:59
  256.6 11.4 %all_gather.41 = bf16[384,768]{0,1:T(8,128)(2,1)S(1)} all-gather(bf16[384,192]{0,1:T(8,128)(2,1)} %reduce-scatter.21.cloned.1.call-done), channel_id=1, replica_groups=mesh['dp'=8,'row'=2,'col'=2] {'row','col'}, dimensions={1}, use_global_device_ids=true | all-gather | bytes 737280 | tf_op jit(solution)/shard_map/all_gather | solution.py:62
  273.8 91.4 %while.37 = (s32[]{:T(128)}, bf16[2,384,4,64]{1,3,2,0:T(8,128)(2,1)S(1)}, bf16[2,384,4,64]{1,3,2,0:T(8,128)(2,1)}, f32[384,4,64]{0,2,1:T(8,128)S(1)}, s32[384]{0...) while((s32[]{:T(128)}, ...), condition=%wide.region_27.28_spmd.clone, body=%wide.region_25.27_spmd.clone.sunk | while | flops 385307520 | bytes 19569080 | solution.py:188
  281.0 11.9 %collective-permute-done.1 = bf16[2,384,4,64]{1,3,2,0:T(8,128)(2,1)S(1)} collective-permute-done((bf16[2,384,4,64]{1,3,2,0:T(8,128)(2,1)S(1)}, bf16[2,384,4,64]{1,3,2,0:T(8,128)(2,1)S(1)}, u32[]{:S(2)}, u32[]{:S(2)}) %collective-permute-start.1) | collective-permute-done | bytes 393248 | tf_op jit(solution)/shard_map/while/body/eval_jaxpr/ppermute | solution.py:18
  306.0 10.3 %collective-permute-done.1 = bf16[2,384,4,64]{1,3,2,0:T(8,128)(2,1)S(1)} collective-permute-done((bf16[2,384,4,64]{1,3,2,0:T(8,128)(2,1)S(1)}, bf16[2,384,4,64]{1,3,2,0:T(8,128)(2,1)S(1)}, u32[]{:S(2)}, u32[]{:S(2)}) %collective-permute-start.1) | collective-permute-done | bytes 393248 | tf_op jit(solution)/shard_map/while/body/eval_jaxpr/ppermute | solution.py:18
  330.3 8.6 %collective-permute-done.1 = bf16[2,384,4,64]{1,3,2,0:T(8,128)(2,1)S(1)} collective-permute-done((bf16[2,384,4,64]{1,3,2,0:T(8,128)(2,1)S(1)}, bf16[2,384,4,64]{1,3,2,0:T(8,128)(2,1)S(1)}, u32[]{:S(2)}, u32[]{:S(2)}) %collective-permute-start.1) | collective-permute-done | bytes 393248 | tf_op jit(solution)/shard_map/while/body/eval_jaxpr/ppermute | solution.py:18
  353.6 7.4 %collective-permute-done.1 = bf16[2,384,4,64]{1,3,2,0:T(8,128)(2,1)S(1)} collective-permute-done((bf16[2,384,4,64]{1,3,2,0:T(8,128)(2,1)S(1)}, bf16[2,384,4,64]{1,3,2,0:T(8,128)(2,1)S(1)}, u32[]{:S(2)}, u32[]{:S(2)}) %collective-permute-start.1) | collective-permute-done | bytes 393248 | tf_op jit(solution)/shard_map/while/body/eval_jaxpr/ppermute | solution.py:18
  371.4 14.7 %collective-permute-done.3 = bf16[2,384,4,64]{1,3,2,0:T(8,128)(2,1)S(1)} collective-permute-done((bf16[2,384,4,64]{1,3,2,0:T(8,128)(2,1)}, bf16[2,384,4,64]{1,3,2,0:T(8,128)(2,1)S(1)}, u32[]{:S(2)}, u32[]{:S(2)}) %collective-permute-start.3) | collective-permute-done | bytes 393248 | tf_op jit(solution)/shard_map/ppermute | solution.py:24
  390.6 20.2 %all-gather.14.cloned.1.call-done = bf16[4,384,768]{2,1,0:T(8,128)(2,1)} async-done(((bf16[1,384,768]{2,1,0:T(8,128)(2,1)}), bf16[4,384,768]{2,1,0:T(8,128)(2,1)}) %all-gather.14.cloned.1.call-update) | async-done | bytes 2359312 | tf_op jit(solution)/shard_map/all_gather | solution.py:302
  438.0 7.8 %all_gather.43 = bf16[384,768]{0,1:T(8,128)(2,1)S(1)} all-gather(bf16[384,192]{0,1:T(8,128)(2,1)} %reduce-scatter.23.cloned.1.call-done), channel_id=1, replica_groups=mesh['dp'=8,'row'=2,'col'=2] {'row','col'}, dimensions={1}, use_global_device_ids=true | all-gather | bytes 737280 | tf_op jit(solution)/shard_map/all_gather | solution.py:62
  447.0 40.8 %all-reduce = (f32[768]{0:T(1024)}, f32[768]{0:T(1024)}, f32[768]{0:T(1024)}, f32[768]{0:T(1024)}, f32[768]{0:T(1024)}, /*index=5*/f32[768]{0:T(1024)}, f32[768]{0:T(1024)}, f32[3072]{0:T(1024)}, f32[768]{0:T(1024)}) all-reduce(f32[768]{0:T(1024)S(1)} %slice.62, f32[768]{0:T(1024)S(1)} %slice.64, ...), channel_id=1, replica_groups=mesh['dp'=8,'row'=2,'col'=2] {'dp'}, use_global_device_ids=true, to_apply=%region_33.34 | all-reduce | flops 9216 | bytes 73728 | tf_op jit(solution)/shard_map/psum | solution.py:315
  489.9 186.1 %all-reduce.4.cloned.1.call-done = (f32[384,1152]{1,0:T(8,128)}, f32[384,384]{1,0:T(8,128)}, f32[384,1536]{1,0:T(8,128)}, f32[1536,384]{1,0:T(8,128)}) async-done(((f32[384,1152]{1,0:T(8,128)}, f32[384,384]{1,0:T(8,128)}, f32[384,1536]{1,0:T(8,128)}, f32[1536,384]{1,0:T(8,128)}), (f32[384,1152]{1,0:T(8,128)}, f32[384,384]{1,0:T(8,128)}, f32[384,1536]{1,0:T(8,128)}, ...) | async-done | bytes 7077904 | tf_op jit(solution)/shard_map/psum | solution.py:315
  (422 shorter events, 224.0 us)
Async XLA Ops:
  8.0 17.8 %reduce-scatter.9.cloned.1.call-start = ((), (), s32[]{:S(2)}) async-start(), calls=%async_computation.8 | async-start | bytes 1327104 | tf_op jit(solution)/shard_map/reduce_scatter | solution.py:45
  14.6 35.6 %all-gather.6.cloned.1.call-start = ((), (), s32[]{:S(2)}) async-start(), calls=%async_computation.9 | async-start | bytes 2211840 | tf_op jit(solution)/shard_map/all_gather | solution.py:51
  27.8 104.3 %reduce-scatter.17.cloned.1.call-start = ((), (), s32[]{:S(2)}) async-start(), calls=%async_computation.14 | async-start | bytes 1769472 | tf_op jit(solution)/shard_map/reduce_scatter | solution.py:59
  38.8 104.8 %reduce-scatter.11.cloned.1.call-start = ((), (), s32[]{:S(2)}) async-start(), calls=%async_computation.10 | async-start | bytes 442368 | tf_op jit(solution)/shard_map/reduce_scatter | solution.py:45
  72.6 12.3 %collective-permute-start = (bf16[2,384,4,64]{1,3,2,0:T(8,128)(2,1)S(1)}, bf16[2,384,4,64]{1,3,2,0:T(8,128)(2,1)S(1)}, u32[]{:S(2)}, u32[]{:S(2)}) collective-permute-start(bf16[2,384,4,64]{1,3,2,0:T(8,128)(2,1)S(1)} %get-tuple-element.799), channel_id=1, source_target_pairs={{0,4},{4,8},{8,12},{12,16},{16,20},{20,24},{24,28},{1,5},{5,9},{9,... | collective-permute-start | bytes 1179656 | tf_op jit(solution)/shard_map/while/body/eval_jaxpr/ppermute | solution.py:18
  132.0 33.5 %all-gather.10.cloned.1.call-start = ((), (), s32[]{:S(2)}) async-start(), calls=%async_computation.15 | async-start | bytes 2949120 | tf_op jit(solution)/shard_map/all_gather | solution.py:62
  132.7 53.6 %reduce-scatter.13.cloned.1.call-start = ((), (), s32[]{:S(2)}) async-start(), calls=%async_computation.11 | async-start | bytes 1769472 | tf_op jit(solution)/shard_map/reduce_scatter | solution.py:45
  159.1 54.8 %all-gather.12.cloned.1.call-start = ((), (), s32[]{:S(2)}) async-start(), calls=%async_computation.16 | async-start | bytes 2949120 | tf_op jit(solution)/shard_map/all_gather | solution.py:51
  189.7 39.0 %reduce-scatter.19.cloned.1.call-start = ((), (), s32[]{:S(2)}) async-start(), calls=%async_computation.17 | async-start | bytes 442368 | tf_op jit(solution)/shard_map/reduce_scatter | solution.py:59
  216.7 39.9 %reduce-scatter.21.cloned.1.call-start = ((), (), s32[]{:S(2)}) async-start(), calls=%async_computation.18 | async-start | bytes 442368 | tf_op jit(solution)/shard_map/reduce_scatter | solution.py:59
  244.1 143.3 %all-gather.8.cloned.1.call-start = ((), (), s32[]{:S(2)}) async-start(), calls=%async_computation.12 | async-start | bytes 2949120 | tf_op jit(solution)/shard_map/all_gather | solution.py:51
  244.7 166.2 %all-gather.14.cloned.1.call-start = ((), (), s32[]{:S(2)}) async-start(), calls=%async_computation.19 | async-start | bytes 2949120 | tf_op jit(solution)/shard_map/all_gather | solution.py:302
  273.8 22.4 %collective-permute-start.2 = (bf16[2,384,4,64]{1,3,2,0:T(8,128)(2,1)}, bf16[2,384,4,64]{1,3,2,0:T(8,128)(2,1)S(1)}, u32[]{:S(2)}, u32[]{:S(2)}) collective-permute-start(bf16[2,384,4,64]{1,3,2,0:T(8,128)(2,1)} %get-tuple-element.850), channel_id=1, source_target_pairs={{28,0},{0,4},{4,8},{8,12},{12,16},{16,20},{20,24},{24,28},{29,1},{... | collective-permute-start | bytes 1179656 | tf_op jit(solution)/shard_map/while/body/eval_jaxpr/ppermute | solution.py:24
  275.3 17.6 %collective-permute-start.1 = (bf16[2,384,4,64]{1,3,2,0:T(8,128)(2,1)S(1)}, bf16[2,384,4,64]{1,3,2,0:T(8,128)(2,1)S(1)}, u32[]{:S(2)}, u32[]{:S(2)}) collective-permute-start(bf16[2,384,4,64]{1,3,2,0:T(8,128)(2,1)S(1)} %get-tuple-element.849), channel_id=1, source_target_pairs={{0,4},{4,8},{8,12},{12,16},{16,20},{20,24},{24,28},{1,5},{5,9},{9,... | collective-permute-start | bytes 1179656 | tf_op jit(solution)/shard_map/while/body/eval_jaxpr/ppermute | solution.py:18
  297.0 22.6 %collective-permute-start.2 = (bf16[2,384,4,64]{1,3,2,0:T(8,128)(2,1)}, bf16[2,384,4,64]{1,3,2,0:T(8,128)(2,1)S(1)}, u32[]{:S(2)}, u32[]{:S(2)}) collective-permute-start(bf16[2,384,4,64]{1,3,2,0:T(8,128)(2,1)} %get-tuple-element.850), channel_id=1, source_target_pairs={{28,0},{0,4},{4,8},{8,12},{12,16},{16,20},{20,24},{24,28},{29,1},{... | collective-permute-start | bytes 1179656 | tf_op jit(solution)/shard_map/while/body/eval_jaxpr/ppermute | solution.py:24
  299.5 16.8 %collective-permute-start.1 = (bf16[2,384,4,64]{1,3,2,0:T(8,128)(2,1)S(1)}, bf16[2,384,4,64]{1,3,2,0:T(8,128)(2,1)S(1)}, u32[]{:S(2)}, u32[]{:S(2)}) collective-permute-start(bf16[2,384,4,64]{1,3,2,0:T(8,128)(2,1)S(1)} %get-tuple-element.849), channel_id=1, source_target_pairs={{0,4},{4,8},{8,12},{12,16},{16,20},{20,24},{24,28},{1,5},{5,9},{9,... | collective-permute-start | bytes 1179656 | tf_op jit(solution)/shard_map/while/body/eval_jaxpr/ppermute | solution.py:18
  320.5 21.7 %collective-permute-start.2 = (bf16[2,384,4,64]{1,3,2,0:T(8,128)(2,1)}, bf16[2,384,4,64]{1,3,2,0:T(8,128)(2,1)S(1)}, u32[]{:S(2)}, u32[]{:S(2)}) collective-permute-start(bf16[2,384,4,64]{1,3,2,0:T(8,128)(2,1)} %get-tuple-element.850), channel_id=1, source_target_pairs={{28,0},{0,4},{4,8},{8,12},{12,16},{16,20},{20,24},{24,28},{29,1},{... | collective-permute-start | bytes 1179656 | tf_op jit(solution)/shard_map/while/body/eval_jaxpr/ppermute | solution.py:24
  322.9 15.9 %collective-permute-start.1 = (bf16[2,384,4,64]{1,3,2,0:T(8,128)(2,1)S(1)}, bf16[2,384,4,64]{1,3,2,0:T(8,128)(2,1)S(1)}, u32[]{:S(2)}, u32[]{:S(2)}) collective-permute-start(bf16[2,384,4,64]{1,3,2,0:T(8,128)(2,1)S(1)} %get-tuple-element.849), channel_id=1, source_target_pairs={{0,4},{4,8},{8,12},{12,16},{16,20},{20,24},{24,28},{1,5},{5,9},{9,... | collective-permute-start | bytes 1179656 | tf_op jit(solution)/shard_map/while/body/eval_jaxpr/ppermute | solution.py:18
  343.0 21.3 %collective-permute-start.2 = (bf16[2,384,4,64]{1,3,2,0:T(8,128)(2,1)}, bf16[2,384,4,64]{1,3,2,0:T(8,128)(2,1)S(1)}, u32[]{:S(2)}, u32[]{:S(2)}) collective-permute-start(bf16[2,384,4,64]{1,3,2,0:T(8,128)(2,1)} %get-tuple-element.850), channel_id=1, source_target_pairs={{28,0},{0,4},{4,8},{8,12},{12,16},{16,20},{20,24},{24,28},{29,1},{... | collective-permute-start | bytes 1179656 | tf_op jit(solution)/shard_map/while/body/eval_jaxpr/ppermute | solution.py:24
  346.1 14.9 %collective-permute-start.1 = (bf16[2,384,4,64]{1,3,2,0:T(8,128)(2,1)S(1)}, bf16[2,384,4,64]{1,3,2,0:T(8,128)(2,1)S(1)}, u32[]{:S(2)}, u32[]{:S(2)}) collective-permute-start(bf16[2,384,4,64]{1,3,2,0:T(8,128)(2,1)S(1)} %get-tuple-element.849), channel_id=1, source_target_pairs={{0,4},{4,8},{8,12},{12,16},{16,20},{20,24},{24,28},{1,5},{5,9},{9,... | collective-permute-start | bytes 1179656 | tf_op jit(solution)/shard_map/while/body/eval_jaxpr/ppermute | solution.py:18
  365.1 20.9 %collective-permute-start.3 = (bf16[2,384,4,64]{1,3,2,0:T(8,128)(2,1)}, bf16[2,384,4,64]{1,3,2,0:T(8,128)(2,1)S(1)}, u32[]{:S(2)}, u32[]{:S(2)}) collective-permute-start(bf16[2,384,4,64]{1,3,2,0:T(8,128)(2,1)} %get-tuple-element.326), channel_id=1, source_target_pairs={{16,0},{20,4},{24,8},{28,12},{0,16},{4,20},{8,24},{12,28},{17,1},{... | collective-permute-start | bytes 1179656 | tf_op jit(solution)/shard_map/ppermute | solution.py:24
  387.3 48.6 %reduce-scatter.15.cloned.1.call-start = ((), (), s32[]{:S(2)}) async-start(), calls=%async_computation.13 | async-start | bytes 442368 | tf_op jit(solution)/shard_map/reduce_scatter | solution.py:45
  390.6 47.4 %reduce-scatter.23.cloned.1.call-start = ((), (), s32[]{:S(2)}) async-start(), calls=%async_computation.20 | async-start | bytes 442368 | tf_op jit(solution)/shard_map/reduce_scatter | solution.py:59
  423.0 253.1 %all-reduce.4.cloned.1.call-start = ((), (), s32[]{:S(2)}) async-start(), calls=%async_computation.21 | async-start | bytes 14155776 | tf_op jit(solution)/shard_map/psum | solution.py:315
  (88 other events, 538.9 us)
Sparse Core Ops, SparseCore 0:
  14.7 11.0 reduce-scatter.8
  28.0 22.1 all-gather.5
  134.4 31.0 all-gather.9
  189.8 24.0 all-gather.11
  246.7 27.6 all-gather.7
  387.4 23.3 all-gather.13
Sparse Core Ops, SparseCore 1:
  38.8 23.3 reduce-scatter.16
  132.1 11.4 reduce-scatter.10
  159.1 10.0 reduce-scatter.12
  216.8 11.9 reduce-scatter.18
  244.1 12.4 reduce-scatter.20
  390.9 6.9 reduce-scatter.14
  423.1 11.9 reduce-scatter.22
  440.5 235.5 all-reduce.3
where the time goes:
time: 703 us; the launch traced here: 692 us
  waiting for transfers between devices  358 us (51%)
  blocking collectives  93.6 us (13%)
  local copies, waits for them, and re-layouts  68.4 us (10%)
  matrix products  58.2 us (8%)
  starting transfers between devices  52.4 us (7%)
  other arithmetic  39 us (6%)
  between operations  16.9 us (2%)
    psum x1, waiting for transfers between devices, shards(): lax.psum((g_down_weight, g_down_bias, g_up_weight, g_up_bias, g_gain_seco...  186 us
    ppermute x8, waiting for transfers between devices, from_behind(): return lax.ppermute(array, axis, pairs)  51.2 us
    psum x1, blocking collectives, shards(): lax.psum((g_down_weight, g_down_bias, g_up_weight, g_up_bias, g_gain_seco...  40.8 us
    ppermute x8, starting transfers between devices, from_behind(): return lax.ppermute(array, axis, pairs)  35.5 us
    all_gather x3, waiting for transfers between devices, spread_low(): return lax.all_gather(share_rows, ('row', 'col'), axis=1, tiled=True)  34.2 us
    all_gather x3, blocking collectives, backward_part(): lax.all_gather(share_rows.astype(jnp.bfloat16), ('row', 'col'), axis=1, t...  26.4 us
    reduce_scatter x4, waiting for transfers between devices, backward_part(): lax.psum_scatter(partial_value.astype(jnp.bfloat16), 'row', scatter_dimen...  23.9 us
    reshape x3, local copies, waits for them, and re-layouts, backward_part(): return pieces.reshape(token_rows, row_count * col_count * share_width)  20.8 us
  transfers between devices with their start and end apart: 27, of which 18 were waited for; matrix products, arithmetic and copies ran while one was open for 18% of the time, Pallas kernels for 0%

commit v1 on v0

v1 whole, which is shorter than its diff:
```python
import functools

import jax
import jax.numpy as jnp
from jax import lax
from jax.experimental import pallas as pl
from jax.experimental.pallas import tpu as pltpu
from jax.sharding import PartitionSpec as P

H = 12
LONGEST = 4096
EPSILON = 1e-05
FLOOR = -1e30
BF = jnp.bfloat16
F32 = jnp.float32
GRID = ("row", "col")
SWAP = [(0, 1), (1, 0)]
TRANSPOSE = [(0, 0), (1, 2), (2, 1), (3, 3)]
TO_FLIPPED = [(0, 1), (1, 3), (2, 0), (3, 2)]
FROM_FLIPPED = [(0, 2), (1, 0), (2, 3), (3, 1)]


def mm(a, b):
    return jnp.dot(a, b, preferred_element_type=F32)


def mm_nt(a, b):
    return lax.dot_general(a, b, (((1,), (1,)), ((), ())), preferred_element_type=F32)


def mm_tn(a, b):
    return lax.dot_general(a, b, (((0,), (0,)), ((), ())), preferred_element_type=F32)


def cut(source, index, extent, axis):
    return lax.dynamic_slice_in_dim(source, index * extent, extent, axis)


def normalise(stream):
    centred = stream - jnp.mean(stream, axis=-1, keepdims=True)
    inverse = lax.rsqrt(jnp.mean(centred * centred, axis=-1, keepdims=True) + EPSILON)
    return centred * inverse, inverse


def smooth_gate(values):
    return jax.nn.gelu(values, approximate=True)


def forward_kernel(base_ref, q_ref, kv_ref, start_ref, out_ref, log_ref, *, heads, size, rows):
    width = heads * size
    keys = kv_ref.shape[0]
    scale = size**-0.5
    first_key = base_ref[0]
    first_query = base_ref[1]

    @pl.loop(0, q_ref.shape[0] // rows)
    def _(block):
        at = pl.ds(pl.multiple_of(block * rows, rows), rows)
        k_pos = first_key + lax.broadcasted_iota(jnp.int32, (rows, keys), 1)
        q_pos = first_query + block * rows + lax.broadcasted_iota(jnp.int32, (rows, keys), 0)
        allowed = (k_pos >= start_ref[at, :]) & (k_pos <= q_pos)
        outs, logs = [], []
        for head in range(heads):
            lo = head * size
            scores = mm_nt(q_ref[at, lo : lo + size], kv_ref[:, lo : lo + size]) * scale
            scores = jnp.where(allowed, scores, FLOOR)
            top = jnp.max(scores, axis=1, keepdims=True)
            weights = jnp.exp(scores - top)
            total = jnp.sum(weights, axis=1, keepdims=True)
            mixed = mm(weights.astype(BF), kv_ref[:, width + lo : width + lo + size])
            outs.append(mixed / total)
            logs.append(top + jnp.log(total))
        out_ref[at, :] = jnp.concatenate(outs, axis=1).astype(BF)
        log_ref[at, :] = jnp.concatenate(logs, axis=1)


def query_kernel(
    base_ref, q_ref, kv_ref, start_ref, log_ref, delta_ref, do_ref, dq_ref, *, heads, size, rows
):
    width = heads * size
    keys = kv_ref.shape[0]
    scale = size**-0.5
    first_key = base_ref[0]
    first_query = base_ref[1]

    @pl.loop(0, q_ref.shape[0] // rows)
    def _(block):
        at = pl.ds(pl.multiple_of(block * rows, rows), rows)
        k_pos = first_key + lax.broadcasted_iota(jnp.int32, (rows, keys), 1)
        q_pos = first_query + block * rows + lax.broadcasted_iota(jnp.int32, (rows, keys), 0)
        allowed = (k_pos >= start_ref[at, :]) & (k_pos <= q_pos)
        outs = []
        for head in range(heads):
            lo = head * size
            keys_here = kv_ref[:, lo : lo + size]
            scores = mm_nt(q_ref[at, lo : lo + size], keys_here) * scale
            scores = jnp.where(allowed, scores, FLOOR)
            weights = jnp.exp(scores - log_ref[at, head : head + 1])
            pulled = mm_nt(do_ref[at, lo : lo + size], kv_ref[:, width + lo : width + lo + size])
            d_scores = weights * (pulled - delta_ref[at, head : head + 1]) * scale
            outs.append(mm(d_scores.astype(BF), keys_here))
        dq_ref[at, :] = jnp.concatenate(outs, axis=1).astype(BF)


def key_kernel(
    base_ref, qo_ref, do_ref, kv_ref, start_ref, log_ref, delta_ref, dkv_ref, *, heads, size, rows
):
    width = heads * size
    queries = qo_ref.shape[0]
    scale = size**-0.5
    first_query = base_ref[0]
    first_key = base_ref[1]

    @pl.loop(0, kv_ref.shape[0] // rows)
    def _(block):
        at = pl.ds(pl.multiple_of(block * rows, rows), rows)
        q_pos = first_query + lax.broadcasted_iota(jnp.int32, (rows, queries), 1)
        k_pos = first_key + block * rows + lax.broadcasted_iota(jnp.int32, (rows, queries), 0)
        allowed = (k_pos >= start_ref[0:1, :]) & (k_pos <= q_pos)
        d_keys, d_values = [], []
        for head in range(heads):
            lo = head * size
            queries_here = qo_ref[:, lo : lo + size]
            d_out = do_ref[:, lo : lo + size]
            scores = mm_nt(kv_ref[at, lo : lo + size], queries_here) * scale
            scores = jnp.where(allowed, scores, FLOOR)
            weights = jnp.exp(scores - log_ref[head : head + 1, :])
            d_values.append(mm(weights.astype(BF), d_out))
            pulled = mm_nt(kv_ref[at, width + lo : width + lo + size], d_out)
            d_scores = weights * (pulled - delta_ref[head : head + 1, :]) * scale
            d_keys.append(mm(d_scores.astype(BF), queries_here))
        dkv_ref[at, :] = jnp.concatenate(d_keys + d_values, axis=1).astype(BF)


def local_kernel(body, out_shape, operands, cost):
    in_vmem = pl.BlockSpec(memory_space=pltpu.VMEM)
    many = isinstance(out_shape, tuple)
    return pl.pallas_call(
        body,
        out_shape=out_shape,
        in_specs=[pl.BlockSpec(memory_space=pltpu.SMEM)] + [in_vmem] * (len(operands) - 1),
        out_specs=(in_vmem,) * len(out_shape) if many else in_vmem,
        compiler_params=pltpu.CompilerParams(vmem_limit_bytes=48 * 1024 * 1024),
        cost_estimate=pl.CostEstimate(
            flops=cost, bytes_accessed=8 << 20, transcendentals=cost // 256
        ),
    )(*operands)


def shards(
    block_in,
    lengths,
    attend_in,
    query_bias,
    value_bias,
    attend_out,
    out_bias,
    gain_first,
    shift_first,
    gain_second,
    shift_second,
    up_weight,
    up_bias,
    down_weight,
    down_bias,
    grad_out,
):
    row = lax.axis_index("row")
    col = lax.axis_index("col")
    place = row * 2 + col
    group = lax.axis_index("dp")
    groups = lax.axis_size("dp")
    tokens, model = block_in.shape
    size = model // H
    heads = H // 4
    share = model // 4
    half = model // 2
    longest = min(LONGEST, tokens * groups // 2)
    visits = min((longest - 2 + tokens) // tokens, groups - 1)
    window = (visits + 1) * tokens
    top = row == 0
    left = col == 0

    crossing = lax.ppermute(attend_in[:, half : 2 * half], "row", SWAP)
    low, high = attend_in[:, :half], attend_in[:, 2 * half :]
    q_half = jnp.where(top, low, crossing)
    k_half = jnp.where(top, high, low)
    v_half = jnp.where(top, crossing, high)
    in_mine = jnp.concatenate([cut(w, col, share, 1) for w in (q_half, k_half, v_half)], axis=1)
    in_other = jnp.concatenate(
        [cut(w, 1 - col, share, 1) for w in (q_half, k_half, v_half)], axis=1
    )
    in_other = lax.ppermute(in_other, "col", SWAP)
    in_own = jnp.concatenate(
        [jnp.where(left, in_mine, in_other), jnp.where(left, in_other, in_mine)], axis=0
    )

    hidden_share = up_weight.shape[1] // 2
    up_mine = cut(up_weight, col, hidden_share, 1)
    up_other = lax.ppermute(cut(up_weight, 1 - col, hidden_share, 1), "col", SWAP)
    up_own = jnp.concatenate(
        [jnp.where(left, up_mine, up_other), jnp.where(left, up_other, up_mine)], axis=0
    )

    def rows_of(at):
        return jnp.concatenate(
            [cut(attend_out, at, share, 0), cut(down_weight, at, hidden_share, 0)], axis=0
        )

    part_a = lax.ppermute(rows_of(row), GRID, TRANSPOSE)
    part_b = lax.ppermute(rows_of(1 - row), GRID, TO_FLIPPED)
    rows_own = jnp.concatenate(
        [jnp.where(left, part_a, part_b), jnp.where(left, part_b, part_a)], axis=1
    )
    out_own, down_own = rows_own[:share], rows_own[share:]
    grad_full = lax.all_gather(grad_out, GRID, axis=1, tiled=True)

    bounds = jnp.cumsum(lengths)
    everywhere = jnp.arange(tokens * groups, dtype=jnp.int32)
    starts = jnp.max(
        jnp.where(bounds[None, :] <= everywhere[:, None], bounds[None, :], 0), axis=1
    )
    start_own = cut(starts, group, tokens, 0)

    stream = block_in.astype(F32)
    n_first, inverse_first = normalise(stream)
    h_first = (n_first * gain_first + shift_first).astype(BF)
    bias_own = jnp.concatenate(
        [
            cut(query_bias, place, share, 0),
            jnp.zeros((share,), F32),
            cut(value_bias, place, share, 0),
        ]
    )
    qkv = (mm(h_first, in_own) + bias_own).astype(BF)
    queries, pair = qkv[:, :share], qkv[:, share:]
    all_pairs = lax.all_gather(pair, "dp", axis=0, tiled=True)
    first_group = jnp.maximum(group - visits, 0)
    pairs = lax.dynamic_slice_in_dim(all_pairs, first_group * tokens, window, 0)
    key_base = jnp.stack([first_group * tokens, group * tokens])
    shape = dict(heads=heads, size=size, rows=128)
    work = 4 * tokens * window * share
    mixed, log_total = local_kernel(
        functools.partial(forward_kernel, **shape),
        (
            jax.ShapeDtypeStruct((tokens, share), BF),
            jax.ShapeDtypeStruct((tokens, heads), F32),
        ),
        (key_base, queries, pairs, start_own[:, None]),
        work,
    )
    branch = lax.psum(mm(mixed, out_own).astype(BF), GRID).astype(F32) + out_bias
    r_first = stream + branch

    n_second, inverse_second = normalise(r_first)
    h_second = (n_second * gain_second + shift_second).astype(BF)
    gate_in = mm(h_second, up_own) + cut(up_bias, place, hidden_share, 0)
    hidden32, gate_pull = jax.vjp(smooth_gate, gate_in)
    hidden = hidden32.astype(BF)
    down_share = lax.psum_scatter(
        mm(hidden, down_own).astype(BF), GRID, scatter_dimension=1, tiled=True
    ).astype(F32)
    block_out = cut(r_first, place, share, 1) + (down_share + cut(down_bias, place, share, 0))

    d_gate = gate_pull(mm_nt(grad_full, down_own))[0].astype(BF)
    d_second = lax.psum(mm_nt(d_gate, up_own).astype(BF), GRID).astype(F32)

    queries_out = lax.all_gather(
        jnp.concatenate([queries, mixed], axis=1), "dp", axis=0, tiled=True
    )
    all_logs = lax.all_gather(log_total, "dp", axis=0, tiled=True)

    acts = jnp.concatenate([hidden, mixed], axis=1)
    acts_a = lax.ppermute(acts, GRID, TRANSPOSE)
    acts_b = lax.ppermute(acts, GRID, FROM_FLIPPED)
    acts_0 = jnp.where(top, acts_a, acts_b)
    acts_1 = jnp.where(top, acts_b, acts_a)
    hidden_half = jnp.concatenate([acts_0[:, :hidden_share], acts_1[:, :hidden_share]], axis=1)
    mixed_half = jnp.concatenate([acts_0[:, hidden_share:], acts_1[:, hidden_share:]], axis=1)
    d_gate_half = lax.all_gather(d_gate, "col", axis=1, tiled=True)

    g_down = mm_tn(hidden_half, cut(grad_full, row, half, 1)).astype(BF)
    g_up = mm_tn(cut(h_second, col, half, 1), d_gate_half).astype(BF)
    g_down, g_up = lax.psum((g_down, g_up), "dp")

    e_second = d_second * gain_second
    d_norm = inverse_second * (
        e_second
        - jnp.mean(e_second, axis=1, keepdims=True)
        - n_second * jnp.mean(e_second * n_second, axis=1, keepdims=True)
    )
    d_r_first = grad_full.astype(F32) + d_norm
    d_branch = d_r_first.astype(BF)
    d_mixed = mm_nt(d_branch, out_own).astype(BF)

    all_d = lax.all_gather(d_mixed, "dp", axis=0, tiled=True)
    delta = jnp.sum(
        (d_mixed.astype(F32) * mixed.astype(F32)).reshape(tokens, heads, size), axis=2
    )
    d_query = local_kernel(
        functools.partial(query_kernel, **shape),
        jax.ShapeDtypeStruct((tokens, share), BF),
        (key_base, queries, pairs, start_own[:, None], log_total, delta, d_mixed),
        6 * tokens * window * share,
    )
    last_start = jnp.minimum(group, groups - 1 - visits) * tokens
    later_qo = lax.dynamic_slice_in_dim(queries_out, last_start, window, 0)
    later_d = lax.dynamic_slice_in_dim(all_d, last_start, window, 0)
    later_log = lax.dynamic_slice_in_dim(all_logs, last_start, window, 0).T
    later_start = lax.dynamic_slice_in_dim(starts, last_start, window, 0)[None, :]
    later_delta = jnp.sum(
        (later_d.astype(F32) * later_qo[:, share:].astype(F32)).reshape(window, heads, size),
        axis=2,
    ).T
    d_pair = local_kernel(
        functools.partial(key_kernel, **shape),
        jax.ShapeDtypeStruct((tokens, 2 * share), BF),
        (
            jnp.stack([last_start, group * tokens]),
            later_qo,
            later_d,
            pair,
            later_start,
            later_log,
            later_delta,
        ),
        8 * tokens * window * share,
    )
    d_keys, d_values = d_pair[:, :share], d_pair[:, share:]
    d_qkv = jnp.concatenate([d_query, d_pair], axis=1)

    d_first = mm_nt(d_qkv, in_own)
    e_part = d_first * gain_first
    stats = jnp.concatenate(
        [
            jnp.sum(e_part, axis=1, keepdims=True),
            jnp.sum(e_part * n_first, axis=1, keepdims=True),
            jnp.zeros((tokens, 62), F32),
        ],
        axis=1,
    )
    sent = jnp.concatenate(
        [
            piece
            for at in range(4)
            for piece in (d_first[:, at * share : (at + 1) * share], stats)
        ],
        axis=1,
    ).astype(BF)
    d_share = lax.psum_scatter(sent, GRID, scatter_dimension=1, tiled=True).astype(F32)
    mean_e = d_share[:, share : share + 1] / model
    mean_en = d_share[:, share + 1 : share + 2] / model
    d_share = d_share[:, :share]
    n_share = cut(n_first, place, share, 1)
    grad_in = (
        cut(d_r_first, place, share, 1)
        + inverse_first * (d_share * cut(gain_first, place, share, 0) - mean_e - n_share * mean_en)
    ).astype(BF)

    moved = lax.ppermute(jnp.where(top, d_values, d_query), "row", SWAP)
    kept = jnp.concatenate(
        [jnp.where(top, d_query, d_keys), moved, jnp.where(top, d_keys, d_values)], axis=1
    )
    both = lax.all_gather(kept, "col", axis=0, tiled=False)
    d_cols = both.reshape(2, tokens, 3, share).transpose(1, 2, 0, 3).reshape(tokens, 3 * half)
    g_in = mm_tn(cut(h_first, col, half, 1), d_cols).astype(BF)
    g_out = mm_tn(mixed_half, cut(d_branch, row, half, 1)).astype(BF)
    g_in, g_out, g_down, g_up = lax.optimization_barrier((g_in, g_out, g_down, g_up))
    g_in, g_out = lax.psum((g_in, g_out), "dp")

    def spread(piece, extent):
        whole = jnp.zeros((extent,), F32)
        return lax.dynamic_update_slice_in_dim(whole, piece, place * piece.shape[0], 0)

    def total(array):
        return jnp.sum(array, axis=0, dtype=F32)

    ours = 0.25
    small = jnp.concatenate(
        [
            spread(total(d_query), model),
            spread(total(d_values), model),
            total(d_branch) * ours,
            spread(total(d_share * n_share), model),
            spread(total(d_share), model),
            total(d_second * n_second) * ours,
            total(d_second) * ours,
            spread(total(d_gate), up_bias.shape[0]),
            total(grad_full) * ours,
        ]
    )
    small = lax.psum(small, ("dp",) + GRID)
    parts = [small[at * model : (at + 1) * model] for at in range(7)]
    g_up_bias = small[7 * model : 7 * model + up_bias.shape[0]]
    g_down_bias = small[7 * model + up_bias.shape[0] :]
    return (
        block_out,
        grad_in,
        g_in.astype(F32),
        parts[0],
        parts[1],
        g_out.astype(F32),
        parts[2],
        parts[3],
        parts[4],
        parts[5],
        parts[6],
        g_up.astype(F32),
        g_up_bias,
        g_down.astype(F32),
        g_down_bias,
    )


def solution(mesh):
    placed = (
        P("dp", None),
        P(),
        P("col", "row"),
        P(),
        P(),
        P("col", "row"),
        P(),
        P(),
        P(),
        P(),
        P(),
        P("col", "row"),
        P(),
        P("col", "row"),
        P(),
        P("dp", ("row", "col")),
    )
    return jax.shard_map(
        shards,
        mesh=mesh,
        in_specs=placed,
        out_specs=(
            P("dp", ("row", "col")),
            P("dp", ("row", "col")),
            P("col", "row"),
            P(),
            P(),
            P("col", "row"),
            P(),
            P(),
            P(),
            P(),
            P(),
            P("col", "row"),
            P(),
            P("col", "row"),
            P(),
        ),
        check_vma=False,
    )
```

time: 703 us -> 573 us (0.82); the launches traced: 692 us -> 571 us
  matrix products: 58.2 us -> 21.2 us
  local copies, waits for them, and re-layouts: 68.4 us -> 35.1 us
  starting transfers between devices: 52.4 us -> 20 us
  Pallas kernels: 0 us -> 19.8 us
  waiting for transfers between devices: 358 us -> 343 us
  blocking collectives: 93.6 us -> 83 us
    ppermute x13 -> x8, waiting for transfers between devices: 65.9 us -> 15.6 us  [the longest x1 8.25 us: shards(): acts_b = lax.ppermute(acts, GRID, FROM_FLIPPED)]
    dot_general x50 -> x12, matrix products: 58.2 us -> 21.2 us  [the longest x4 7.8 us: mm_tn(): lax.dot_general(a, b, (((0,), (0,)), ((), ())), preferred_element_type=F32)]
    ppermute x13 -> x8, starting transfers between devices: 51.3 us -> 19.4 us  [the longest x1 7.3 us: shards(): part_a = lax.ppermute(rows_of(row), GRID, TRANSPOSE)]
    psum x1 -> x4, waiting for transfers between devices: 186 us -> 214 us  [the longest x1 84.1 us: shards(): g_down, g_up = lax.psum((g_down, g_up), 'dp')]
    reduce_scatter x8 -> x1, waiting for transfers between devices: 44.6 us -> 21.7 us  [shards(): lax.psum_scatter(sent, GRID, scatter_dimension=1, tiled=True).astype(F32)]
    reshape x4 -> x1, local copies, waits for them, and re-layouts: 21.6 us -> 0.2 us  [shards(): both.reshape(2, tokens, 3, share).transpose(1, 2, 0, 3)]
    pallas_call x0 -> x3, Pallas kernels: none -> 19.8 us  [local_kernel(): pl.pallas_call(body, out_shape=out_shape, in_specs=[pl.BlockSpec(memory_s...]
    unnamed x14 -> x11, waiting for transfers between devices: 1.35 us -> 19.2 us
  transfers between devices with their start and end apart: 27 -> 18, of which waited for: 18 -> 13; matrix products, arithmetic and copies ran while one was open for 18% -> 12% of each run, Pallas kernels for 0% -> 3%
where the time goes in v1:
time: 573 us; the launch traced here: 571 us
  waiting for transfers between devices  343 us (60%)
  blocking collectives  83 us (14%)
  local copies, waits for them, and re-layouts  35.1 us (6%)
  other arithmetic  33.5 us (6%)
  matrix products  21.2 us (4%)
  starting transfers between devices  20 us (3%)
  Pallas kernels  19.8 us (3%)
  between operations  14.9 us (3%)
    psum x1, waiting for transfers between devices, shards(): g_down, g_up = lax.psum((g_down, g_up), 'dp')  84.1 us
    psum x1, waiting for transfers between devices, shards(): g_in, g_out = lax.psum((g_in, g_out), 'dp')  78 us
    psum x1, blocking collectives, shards(): small = lax.psum(small, ('dp',) + GRID)  39.7 us
    all_gather x1, waiting for transfers between devices, shards(): all_pairs = lax.all_gather(pair, 'dp', axis=0, tiled=True)  39.1 us
    all_gather x1, waiting for transfers between devices, shards(): lax.all_gather(jnp.concatenate([queries, mixed], axis=1), 'dp', axis=0, t...  33.3 us
    psum x1, waiting for transfers between devices, shards(): d_second = lax.psum(mm_nt(d_gate, up_own).astype(BF), GRID).astype(F32)  32.3 us
    all_gather x1, blocking collectives, shards(): all_logs = lax.all_gather(log_total, 'dp', axis=0, tiled=True)  31.5 us
    reduce_scatter x1, waiting for transfers between devices, shards(): lax.psum_scatter(sent, GRID, scatter_dimension=1, tiled=True).astype(F32)  21.7 us
  transfers between devices with their start and end apart: 18, of which 13 were waited for; matrix products, arithmetic and copies ran while one was open for 12% of the time, Pallas kernels for 3%

profile of v1, /device:TPU:0, one launch (start us, length us, event | category | flops | bytes accessed | tf_op | source)
XLA Modules:
  0.0 570.5 jit_solution(14602030584745805291)
XLA Ops:
  8.3 3.0 collective-permute-start
  14.5 3.8 collective-permute-done
  25.8 7.3 %collective-permute-start.2 = (bf16[960,384]{1,0:T(8,128)(2,1)}, bf16[960,384]{1,0:T(8,128)(2,1)}, u32[]{:S(2)}, u32[]{:S(2)}) collective-permute-start(bf16[960,384]{1,0:T(8,128)(2,1)} %pad_maximum_fusion.6), channel_id=1, source_target_pairs={{0,0},{1,2},{2,1},{3,3},{4,4},{5,6},{6,5},{7,7},{8,8},{9,10},{10,9... | collective-permute-start | bytes 2211848 | tf_op jit(solution)/shard_map/ppermute | solution.py:210
  38.6 39.1 %all-gather.6.cloned.1.call-done = bf16[3072,384]{1,0:T(8,128)(2,1)} async-done(((bf16[384,384]{1,0:T(8,128)(2,1)}), bf16[3072,384]{1,0:T(8,128)(2,1)}) %all-gather.6.cloned.1.call-update) | async-done | bytes 2359312 | tf_op jit(solution)/shard_map/all_gather | solution.py:237
  79.2 6.4 %shard_map.271 = (bf16[384,192]{1,0:T(8,128)(2,1)S(1)}, f32[384,3]{1,0:T(8,128)S(1)}) custom-call(s32[2]{0:T(128)S(1)} %pad_add_fusion.base_ref, bf16[384,192]{1,0:T(8,128)(2,1)S(1)} %slice.124.q_ref, bf16[1920,384]{1,0:T(8,128)(2,1)S(1)} %constant_dynamic-slice_fusion.7.kv_ref, s32[384,1]{1,0:T(8,128)S(1)} %broadcast_in_dim.32.start_ref), custom_call_target="tpu_custom_call" | custom-call | flops 566231040 | bytes 8388608 | tf_op jit(solution)/shard_map/pallas_call | solution.py:138
  86.9 9.1 %all_gather.25 = bf16[384,768]{0,1:T(8,128)(2,1)} all-gather(bf16[384,192]{0,1:T(8,128)(2,1)S(1)} %copy-done.39), channel_id=1, replica_groups=mesh['dp'=8,'row'=2,'col'=2] {'row','col'}, dimensions={1}, use_global_device_ids=true | all-gather | bytes 737280 | tf_op jit(solution)/shard_map/all_gather | solution.py:216
  99.2 19.8 %all-reduce.7.cloned.1.call-done = bf16[384,768]{1,0:T(8,128)(2,1)} async-done(((bf16[384,768]{1,0:T(8,128)(2,1)}), bf16[384,768]{1,0:T(8,128)(2,1)}) %all-reduce.7.cloned.1.call-update) | async-done | bytes 589840 | tf_op jit(solution)/shard_map/psum | solution.py:252
  125.9 2.9 convolution_convert_fusion.3
  130.1 32.3 %all-reduce.9.cloned.1.call-done = bf16[384,768]{1,0:T(8,128)(2,1)} async-done(((bf16[384,768]{1,0:T(8,128)(2,1)}), bf16[384,768]{1,0:T(8,128)(2,1)}) %all-reduce.9.cloned.1.call-update) | async-done | bytes 589840 | tf_op jit(solution)/shard_map/psum | solution.py:266
  164.6 2.9 convert_reduce_fusion.4
  173.2 7.3 %collective-permute-start.6 = (bf16[384,960]{0,1:T(8,128)(2,1)}, bf16[384,960]{0,1:T(8,128)(2,1)}, u32[]{:S(2)}, u32[]{:S(2)}) collective-permute-start(bf16[384,960]{0,1:T(8,128)(2,1)} %copy.103), channel_id=1, source_target_pairs={{0,0},{1,2},{2,1},{3,3},{4,4},{5,6},{6,5},{7,7},{8,8},{9,10},{10,9... | collective-permute-start | bytes 2211848 | tf_op jit(solution)/shard_map/ppermute | solution.py:274
  180.4 8.3 %collective-permute-done.7 = bf16[384,960]{0,1:T(8,128)(2,1)S(1)} collective-permute-done((bf16[384,960]{0,1:T(8,128)(2,1)}, bf16[384,960]{0,1:T(8,128)(2,1)S(1)}, u32[]{:S(2)}, u32[]{:S(2)}) %collective-permute-start.7) | collective-permute-done | bytes 737312 | tf_op jit(solution)/shard_map/ppermute | solution.py:275
  193.5 3.1 convolution_convert_fusion.1
  197.0 31.5 %all_gather.28 = f32[3072,3]{0,1:T(4,128)S(1)} all-gather(f32[384,3]{0,1:T(4,128)S(1)} %copy.91), channel_id=1, replica_groups=mesh['dp'=8,'row'=2,'col'=2] {'dp'}, dimensions={0}, use_global_device_ids=true | all-gather | bytes 41472 | tf_op jit(solution)/shard_map/all_gather | solution.py:271
  228.4 3.0 fusion.6
  232.9 6.2 %shard_map.272 = bf16[384,192]{1,0:T(8,128)(2,1)S(1)} custom-call(s32[2]{0:T(128)S(1)} %pad_add_fusion.base_ref, bf16[384,192]{1,0:T(8,128)(2,1)S(1)} %slice.124.q_ref, bf16[1920,384]{1,0:T(8,128)(2,1)S(1)} %constant_dynamic-slice_fusion.7.kv_ref, s32[384,1]{1,0:T(8,128)S(1)} %broadcast_in_dim.32.start_ref, f32[384,3]{1,0:T(8,128)S(1)} %get-tuple-element.22.log_ref, ...), custom_call_target="tpu_custom_call" | custom-call | flops 849346560 | bytes 8388608 | tf_op jit(solution)/shard_map/pallas_call | solution.py:138
  240.5 33.3 %all-gather.8.cloned.1.call-done = bf16[3072,384]{1,0:T(8,128)(2,1)} async-done(((bf16[384,384]{1,0:T(8,128)(2,1)}), bf16[3072,384]{1,0:T(8,128)(2,1)}) %all-gather.8.cloned.1.call-update) | async-done | bytes 2359312 | tf_op jit(solution)/shard_map/all_gather | solution.py:268
  273.8 3.3 convert_multiply_fusion
  281.5 7.2 %shard_map.273 = bf16[384,384]{1,0:T(8,128)(2,1)S(1)} custom-call(s32[2]{0:T(128)S(1)} %pad_add_fusion.1.base_ref, bf16[1920,384]{1,0:T(8,128)(2,1)S(1)} %constant_dynamic-slice_fusion.1.qo_ref, bf16[1920,192]{1,0:T(8,128)(2,1)S(1)} %constant_dynamic-slice_fusion.do_ref, bf16[384,384]{1,0:T(8,128)(2,1)S(1)} %copy-done, ...), custom_call_target="tpu_custom_call" | custom-call | flops 1132462080 | bytes 8388608 | tf_op jit(solution)/shard_map/pallas_call | solution.py:138
  301.0 84.1 %all-reduce.13.cloned.1.call-done = (bf16[1536,384]{1,0:T(8,128)(2,1)}, bf16[384,1536]{1,0:T(8,128)(2,1)}) async-done(((bf16[1536,384]{1,0:T(8,128)(2,1)}, bf16[384,1536]{1,0:T(8,128)(2,1)}), (bf16[1536,384]{1,0:T(8,128)(2,1)}, bf16[384,1536]{1,0:T(8,128)(2,1)})) %all-reduce.13.cloned.1.call-update) | async-done | bytes 2359312 | tf_op jit(solution)/shard_map/psum | solution.py:284
  389.9 19.0 %reduce-scatter.7.cloned.1.call-done = bf16[192,384]{1,0:T(8,128)(2,1)} async-done(((bf16[768,384]{1,0:T(8,128)(2,1)}), bf16[192,384]{1,0:T(8,128)(2,1)}) %reduce-scatter.7.cloned.1.call-update) | async-done | bytes 147472
  415.7 78.0 %all-reduce.11.cloned.1.call-done = (bf16[384,1152]{1,0:T(8,128)(2,1)}, bf16[384,384]{1,0:T(8,128)(2,1)}) async-done(((bf16[384,1152]{1,0:T(8,128)(2,1)}, bf16[384,384]{1,0:T(8,128)(2,1)}), (bf16[384,1152]{1,0:T(8,128)(2,1)}, bf16[384,384]{1,0:T(8,128)(2,1)})) %all-reduce.11.cloned.1.call-update) | async-done | bytes 1179664 | tf_op jit(solution)/shard_map/psum | solution.py:369
  496.9 21.7 %reduce-scatter.5.cloned.1.call-done = bf16[384,256]{1,0:T(8,128)(2,1)} async-done(((bf16[384,1024]{1,0:T(8,128)(2,1)}), bf16[384,256]{1,0:T(8,128)(2,1)}) %reduce-scatter.5.cloned.1.call-update) | async-done | bytes 196624 | tf_op jit(solution)/shard_map/reduce_scatter | solution.py:350
  522.0 39.7 %psum.54 = f32[9216]{0:T(1024)S(1)} all-reduce(f32[9216]{0:T(1024)S(1)} %constant_dynamic-update-slice_fusion), channel_id=1, replica_groups=mesh['dp'=8,'row'=2,'col'=2] {'dp','row','col'}, use_global_device_ids=true, to_apply=%region_28.29 | all-reduce | flops 9216 | bytes 73728 | tf_op jit(solution)/shard_map/psum | solution.py:392
  (243 shorter events, 83.5 us)
Async XLA Ops:
  7.2 70.5 %all-gather.6.cloned.1.call-start = ((), (), s32[]{:S(2)}) async-start(), calls=%async_computation.2 | async-start | bytes 2654208 | tf_op jit(solution)/shard_map/all_gather | solution.py:237
  8.3 10.0 %collective-permute-start = (bf16[384,384]{1,0:T(8,128)(2,1)S(1)}, bf16[384,384]{1,0:T(8,128)(2,1)S(1)}, u32[]{:S(2)}, u32[]{:S(2)}) collective-permute-start(bf16[384,384]{1,0:T(8,128)(2,1)S(1)} %slice.95), channel_id=1, source_target_pairs={{0,2},{2,0},{1,3},{3,1},{4,6},{6,4},{5,7},{7,5},{8,10},{10,8},{9,1... | collective-permute-start | bytes 884744 | tf_op jit(solution)/shard_map/ppermute | solution.py:184
  19.2 1.9 collective-permute-start.1
  24.0 95.0 %all-reduce.7.cloned.1.call-start = ((), (), s32[]{:S(2)}) async-start(), calls=%async_computation.3 | async-start | bytes 1179648 | tf_op jit(solution)/shard_map/psum | solution.py:252
  24.7 11.5 %collective-permute-start.3 = (bf16[960,384]{1,0:T(8,128)(2,1)S(1)}, bf16[960,384]{1,0:T(8,128)(2,1)S(1)}, u32[]{:S(2)}, u32[]{:S(2)}) collective-permute-start(bf16[960,384]{1,0:T(8,128)(2,1)S(1)} %pad_maximum_fusion.7), channel_id=1, source_target_pairs={{0,1},{1,3},{2,0},{3,2},{4,5},{5,7},{6,4},{7,6},{8,9},{9,11},{10,8... | collective-permute-start | bytes 2211848 | tf_op jit(solution)/shard_map/ppermute | solution.py:211
  25.8 10.4 %collective-permute-start.2 = (bf16[960,384]{1,0:T(8,128)(2,1)}, bf16[960,384]{1,0:T(8,128)(2,1)}, u32[]{:S(2)}, u32[]{:S(2)}) collective-permute-start(bf16[960,384]{1,0:T(8,128)(2,1)} %pad_maximum_fusion.6), channel_id=1, source_target_pairs={{0,0},{1,2},{2,1},{3,3},{4,4},{5,6},{6,5},{7,7},{8,8},{9,10},{10,9... | collective-permute-start | bytes 2211848 | tf_op jit(solution)/shard_map/ppermute | solution.py:210
  34.0 62.8 %collective-permute-start.4 = (bf16[384,768]{1,0:T(8,128)(2,1)}, bf16[384,768]{1,0:T(8,128)(2,1)}, u32[]{:S(2)}, u32[]{:S(2)}) collective-permute-start(bf16[384,768]{1,0:T(8,128)(2,1)} %constant_dynamic-slice_fusion.2), channel_id=1, source_target_pairs={{0,1},{1,0},{2,3},{3,2},{4,5},{5,4},{6,7},{7,6},{8,9},{9,8},{10,11... | collective-permute-start | bytes 1769480 | tf_op jit(solution)/shard_map/ppermute | solution.py:200
  86.8 75.6 %all-reduce.9.cloned.1.call-start = ((), (), s32[]{:S(2)}) async-start(), calls=%async_computation.4 | async-start | bytes 1179648 | tf_op jit(solution)/shard_map/psum | solution.py:266
  128.8 64.8 %all-gather.12.cloned.1.call-start = ((), (), s32[]{:S(2)}) async-start(), calls=%async_computation.8 | async-start | bytes 1769472 | tf_op jit(solution)/shard_map/all_gather | solution.py:280
  129.9 109.2 %all-gather.10.cloned.1.call-start = ((), (), s32[]{:S(2)}) async-start(), calls=%async_computation.6 | async-start | bytes 1769472 | tf_op jit(solution)/shard_map/all_gather | solution.py:296
  168.7 105.1 %all-gather.8.cloned.1.call-start = ((), (), s32[]{:S(2)}) async-start(), calls=%async_computation.5 | async-start | bytes 2654208 | tf_op jit(solution)/shard_map/all_gather | solution.py:268
  169.6 215.5 %all-reduce.13.cloned.1.call-start = ((), (), s32[]{:S(2)}) async-start(), calls=%async_computation.11 | async-start | bytes 4718592 | tf_op jit(solution)/shard_map/psum | solution.py:284
  173.1 15.6 %collective-permute-start.7 = (bf16[384,960]{0,1:T(8,128)(2,1)}, bf16[384,960]{0,1:T(8,128)(2,1)S(1)}, u32[]{:S(2)}, u32[]{:S(2)}) collective-permute-start(bf16[384,960]{0,1:T(8,128)(2,1)} %copy.103), channel_id=1, source_target_pairs={{0,2},{1,0},{2,3},{3,1},{4,6},{5,4},{6,7},{7,5},{8,10},{9,8},{10,1... | collective-permute-start | bytes 2211848 | tf_op jit(solution)/shard_map/ppermute | solution.py:275
  173.2 15.5 %collective-permute-start.6 = (bf16[384,960]{0,1:T(8,128)(2,1)}, bf16[384,960]{0,1:T(8,128)(2,1)}, u32[]{:S(2)}, u32[]{:S(2)}) collective-permute-start(bf16[384,960]{0,1:T(8,128)(2,1)} %copy.103), channel_id=1, source_target_pairs={{0,0},{1,2},{2,1},{3,3},{4,4},{5,6},{6,5},{7,7},{8,8},{9,10},{10,9... | collective-permute-start | bytes 2211848 | tf_op jit(solution)/shard_map/ppermute | solution.py:274
  196.6 31.8 %copy-start.7 = (bf16[960,384]{1,0:T(8,128)(2,1)S(1)}, bf16[960,384]{1,0:T(8,128)(2,1)}, u32[]{:S(2)}) copy-start(bf16[960,384]{1,0:T(8,128)(2,1)} %copy-done.5) | copy-start | bytes 2211844
  196.7 212.2 %reduce-scatter.7.cloned.1.call-start = ((), (), s32[]{:S(2)}) async-start(), calls=%async_computation.9 | async-start | bytes 737280
  231.4 262.3 %all-reduce.11.cloned.1.call-start = ((), (), s32[]{:S(2)}) async-start(), calls=%async_computation.10 | async-start | bytes 2359296 | tf_op jit(solution)/shard_map/psum | solution.py:369
  239.1 34.7 %copy-start.13 = (bf16[3072,192]{1,0:T(8,128)(2,1)S(1)}, bf16[3072,192]{1,0:T(8,128)(2,1)}, u32[]{:S(2)}) copy-start(bf16[3072,192]{1,0:T(8,128)(2,1)} %all-gather.10.cloned.1.call-done) | copy-start | bytes 3538948
  288.9 5.7 %collective-permute-start.5 = (bf16[384,192]{1,0:T(8,128)(2,1)S(1)}, bf16[384,192]{1,0:T(8,128)(2,1)S(1)}, u32[]{:S(2)}, u32[]{:S(2)}) collective-permute-start(bf16[384,192]{1,0:T(8,128)(2,1)S(1)} %get-tuple-element.128), channel_id=1, source_target_pairs={{0,2},{2,0},{1,3},{3,1},{4,6},{6,4},{5,7},{7,5},{8,10},{10,8},{9,1... | collective-permute-start | bytes 442376 | tf_op jit(solution)/shard_map/ppermute | solution.py:360
  299.4 85.8 %copy-start.4 = (bf16[384,768]{1,0:T(8,128)(2,1)S(1)}, bf16[384,768]{1,0:T(8,128)(2,1)}, u32[]{:S(2)}) copy-start(bf16[384,768]{1,0:T(8,128)(2,1)} %param.16) | copy-start | bytes 1769476
  299.4 85.8 %copy-start.35 = (bf16[384,576]{1,0:T(8,128)(2,1)S(1)}, bf16[384,576]{1,0:T(8,128)(2,1)}, u32[]{:S(2)}) copy-start(bf16[384,576]{1,0:T(8,128)(2,1)} %copy-done.34) | copy-start | bytes 1327108
  299.4 85.8 %copy-start.37 = (bf16[384,576]{1,0:T(8,128)(2,1)S(1)}, bf16[384,576]{1,0:T(8,128)(2,1)}, u32[]{:S(2)}) copy-start(bf16[384,576]{1,0:T(8,128)(2,1)} %copy-done.36) | copy-start | bytes 1327108
  385.1 133.6 %reduce-scatter.5.cloned.1.call-start = ((), (), s32[]{:S(2)}) async-start(), calls=%async_computation.7 | async-start | bytes 983040 | tf_op jit(solution)/shard_map/reduce_scatter | solution.py:350
  389.5 22.9 %copy-start.25 = (bf16[384,1536]{1,0:T(8,128)(2,1)S(1)}, bf16[384,1536]{1,0:T(8,128)(2,1)}, u32[]{:S(2)}) copy-start(bf16[384,1536]{1,0:T(8,128)(2,1)} %get-tuple-element.25) | copy-start | bytes 3538948
  (40 other events, 113.7 us)
Sparse Core Ops, SparseCore 0:
  24.1 53.5 all-gather.5
  86.9 32.0 all-reduce.6
  128.9 33.4 all-reduce.8
  163.8 9.2 all-gather.11
  175.1 45.5 all-gather.9
  222.7 51.0 all-gather.7
  277.4 107.6 all-reduce.12
  387.7 21.0 reduce-scatter.6
  413.4 80.2 all-reduce.10
  496.1 22.5 reduce-scatter.4

commit v2 on v1

--- a/solution.py
+++ b/solution.py
@@ -145,6 +145,183 @@
             flops=cost, bytes_accessed=8 << 20, transcendentals=cost // 256
         ),
     )(*operands)
+
+
+def exchange(source, slots, result, sems, peers, me, count, axis):
+    chunk = source.shape[0] // count
+    send_one, recv_one, send_two, recv_two = sems
+
+    def rows_at(index):
+        return pl.ds(pl.multiple_of(index * chunk, chunk), chunk)
+
+    first, second = [], []
+    for k in range(1, count):
+        first.append(
+            pltpu.make_async_remote_copy(
+                src_ref=source.at[rows_at(lax.rem(me + k, count))],
+                dst_ref=slots.at[k - 1],
+                send_sem=send_one.at[k - 1],
+                recv_sem=recv_one.at[k - 1],
+                device_id=peers(k),
+                device_id_type=pl.DeviceIdType.MESH,
+            )
+        )
+        second.append(
+            pltpu.make_async_remote_copy(
+                src_ref=result.at[rows_at(me)],
+                dst_ref=result.at[rows_at(me)],
+                send_sem=send_two.at[k - 1],
+                recv_sem=recv_two.at[k - 1],
+                device_id=peers(k),
+                device_id_type=pl.DeviceIdType.MESH,
+            )
+        )
+    return first, second, rows_at(me)
+
+
+def greet(devices):
+    barrier = pltpu.get_barrier_semaphore()
+    for device in devices:
+        pl.semaphore_signal(
+            barrier, inc=1, device_id=device, device_id_type=pl.DeviceIdType.MESH
+        )
+    pl.semaphore_wait(barrier, len(devices))
+
+
+def grid_device(k):
+    place = lax.rem(lax.axis_index("row") * 2 + lax.axis_index("col") + k, 4)
+    return {"row": place // 2, "col": lax.rem(place, 2)}
+
+
+def grid_sum_kernel(source, result, slots, *sems):
+    place = lax.axis_index("row") * 2 + lax.axis_index("col")
+    greet([grid_device(k) for k in range(1, 4)])
+    first, second, mine = exchange(source, slots, result, sems, grid_device, place, 4, GRID)
+    for copy in first:
+        copy.start()
+    for copy in first:
+        copy.wait()
+    summed = source[mine, :].astype(F32)
+    for k in range(3):
+        summed = summed + slots[k].astype(F32)
+    result[mine, :] = summed.astype(BF)
+    for copy in second:
+        copy.start()
+    for copy in second:
+        copy.wait()
+
+
+def grid_sum(partial_value, collective_id):
+    rows, columns = partial_value.shape
+    in_vmem = pl.BlockSpec(memory_space=pltpu.VMEM)
+    return pl.pallas_call(
+        grid_sum_kernel,
+        out_shape=jax.ShapeDtypeStruct((rows, columns), BF),
+        in_specs=[in_vmem],
+        out_specs=in_vmem,
+        scratch_shapes=[pltpu.VMEM((3, rows // 4, columns), BF)]
+        + [pltpu.SemaphoreType.DMA((3,))] * 4,
+        compiler_params=pltpu.CompilerParams(
+            collective_id=collective_id,
+            has_side_effects=True,
+            vmem_limit_bytes=24 * 1024 * 1024,
+        ),
+        cost_estimate=pl.CostEstimate(
+            flops=4 * rows * columns, bytes_accessed=24 << 20, transcendentals=0
+        ),
+    )(partial_value)
+
+
+def group_sum_kernel(count, source, small, result, small_out, slots, small_slots, total, *sems):
+    group = lax.axis_index("dp")
+    place = lax.axis_index("row") * 2 + lax.axis_index("col")
+
+    def peers(k):
+        return {"dp": lax.rem(group + k, count)}
+
+    greet([peers(k) for k in range(1, count)] + [grid_device(k) for k in range(1, 4)])
+    first, second, mine = exchange(source, slots, result, sems[:4], peers, group, count, "dp")
+    send_small, recv_small, send_grid, recv_grid = sems[4:]
+    small_first = [
+        pltpu.make_async_remote_copy(
+            src_ref=small,
+            dst_ref=small_slots.at[k - 1],
+            send_sem=send_small.at[k - 1],
+            recv_sem=recv_small.at[k - 1],
+            device_id=peers(k),
+            device_id_type=pl.DeviceIdType.MESH,
+        )
+        for k in range(1, count)
+    ]
+    small_second = [
+        pltpu.make_async_remote_copy(
+            src_ref=total,
+            dst_ref=small_out.at[place],
+            send_sem=send_grid.at[k - 1],
+            recv_sem=recv_grid.at[k - 1],
+            device_id=grid_device(k),
+            device_id_type=pl.DeviceIdType.MESH,
+        )
+        for k in range(1, 4)
+    ]
+    for copy in small_first + first:
+        copy.start()
+    for copy in small_first:
+        copy.wait()
+    gathered = jnp.zeros(small.shape, F32)
+    for at in range(count):
+        back = lax.rem(group - at + count, count)
+        other = small_slots[jnp.maximum(back - 1, 0)]
+        gathered = gathered + jnp.where(back == 0, small[...], other)
+    total[...] = gathered
+    small_out[place] = gathered
+    for copy in small_second:
+        copy.start()
+    for copy in first:
+        copy.wait()
+    summed = source[mine, :].astype(F32)
+    for k in range(count - 1):
+        summed = summed + slots[k].astype(F32)
+    result[mine, :] = summed.astype(BF)
+    for copy in second:
+        copy.start()
+    for copy in small_second + second:
+        copy.wait()
+
+
+def group_sum(grads, small, groups):
+    rows, columns = grads.shape
+    if groups > 8 or rows % (16 * groups):
+        return lax.psum(grads, "dp"), lax.all_gather(lax.psum(small, "dp"), GRID)
+    in_vmem = pl.BlockSpec(memory_space=pltpu.VMEM)
+    return pl.pallas_call(
+        functools.partial(group_sum_kernel, groups),
+        out_shape=(
+            jax.ShapeDtypeStruct(grads.shape, BF),
+            jax.ShapeDtypeStruct((4,) + small.shape, F32),
+        ),
+        in_specs=[in_vmem] * 2,
+        out_specs=(in_vmem, in_vmem),
+        scratch_shapes=[
+            pltpu.VMEM((groups - 1, rows // groups, columns), BF),
+            pltpu.VMEM((groups - 1,) + small.shape, F32),
+            pltpu.VMEM(small.shape, F32),
+        ]
+        + [pltpu.SemaphoreType.DMA((groups - 1,))] * 6
+        + [pltpu.SemaphoreType.DMA((3,))] * 2,
+        compiler_params=pltpu.CompilerParams(
+            collective_id=3, has_side_effects=True, vmem_limit_bytes=24 * 1024 * 1024
+        ),
+        cost_estimate=pl.CostEstimate(
+            flops=8 * rows * columns, bytes_accessed=100 << 20, transcendentals=0
+        ),
+    )(grads, small)
+
+
+def from_behind(array, by, groups):
+    return lax.ppermute(
+        array, "dp", [(i, i + by) for i in range(groups) if 0 <= i + by < groups]
+    )
 
 
 def shards(
@@ -234,10 +411,10 @@
     )
     qkv = (mm(h_first, in_own) + bias_own).astype(BF)
     queries, pair = qkv[:, :share], qkv[:, share:]
-    all_pairs = lax.all_gather(pair, "dp", axis=0, tiled=True)
-    first_group = jnp.maximum(group - visits, 0)
-    pairs = lax.dynamic_slice_in_dim(all_pairs, first_group * tokens, window, 0)
-    key_base = jnp.stack([first_group * tokens, group * tokens])
+    pairs = jnp.concatenate(
+        [from_behind(pair, by, groups) for by in range(visits, 0, -1)] + [pair], axis=0
+    )
+    key_base = jnp.stack([(group - visits) * tokens, group * tokens])
     shape = dict(heads=heads, size=size, rows=128)
     work = 4 * tokens * window * share
     mixed, log_total = local_kernel(
@@ -249,7 +426,7 @@
         (key_base, queries, pairs, start_own[:, None]),
         work,
     )
-    branch = lax.psum(mm(mixed, out_own).astype(BF), GRID).astype(F32) + out_bias
+    branch = grid_sum(mm(mixed, out_own).astype(BF), 1).astype(F32) + out_bias
     r_first = stream + branch
 
     n_second, inverse_second = normalise(r_first)
@@ -263,12 +440,20 @@
     block_out = cut(r_first, place, share, 1) + (down_share + cut(down_bias, place, share, 0))
 
     d_gate = gate_pull(mm_nt(grad_full, down_own))[0].astype(BF)
-    d_second = lax.psum(mm_nt(d_gate, up_own).astype(BF), GRID).astype(F32)
-
-    queries_out = lax.all_gather(
-        jnp.concatenate([queries, mixed], axis=1), "dp", axis=0, tiled=True
-    )
-    all_logs = lax.all_gather(log_total, "dp", axis=0, tiled=True)
+    d_second = grid_sum(mm_nt(d_gate, up_own).astype(BF), 2).astype(F32)
+
+    own_qo = jnp.concatenate([queries, mixed], axis=1)
+    later_qo = jnp.concatenate(
+        [own_qo] + [from_behind(own_qo, -by, groups) for by in range(1, visits + 1)], axis=0
+    )
+    own_log = log_total.T
+    later_log = jnp.concatenate(
+        [own_log] + [from_behind(own_log, -by, groups) for by in range(1, visits + 1)], axis=1
+    )
+    beyond = jnp.full((tokens * visits,), tokens * groups, jnp.int32)
+    later_start = lax.dynamic_slice_in_dim(
+        jnp.concatenate([starts, beyond]), group * tokens, window, 0
+    )[None, :]
 
     acts = jnp.concatenate([hidden, mixed], axis=1)
     acts_a = lax.ppermute(acts, GRID, TRANSPOSE)
@@ -293,7 +478,9 @@
     d_branch = d_r_first.astype(BF)
     d_mixed = mm_nt(d_branch, out_own).astype(BF)
 
-    all_d = lax.all_gather(d_mixed, "dp", axis=0, tiled=True)
+    later_d = jnp.concatenate(
+        [d_mixed] + [from_behind(d_mixed, -by, groups) for by in range(1, visits + 1)], axis=0
+    )
     delta = jnp.sum(
         (d_mixed.astype(F32) * mixed.astype(F32)).reshape(tokens, heads, size), axis=2
     )
@@ -303,11 +490,6 @@
         (key_base, queries, pairs, start_own[:, None], log_total, delta, d_mixed),
         6 * tokens * window * share,
     )
-    last_start = jnp.minimum(group, groups - 1 - visits) * tokens
-    later_qo = lax.dynamic_slice_in_dim(queries_out, last_start, window, 0)
-    later_d = lax.dynamic_slice_in_dim(all_d, last_start, window, 0)
-    later_log = lax.dynamic_slice_in_dim(all_logs, last_start, window, 0).T
-    later_start = lax.dynamic_slice_in_dim(starts, last_start, window, 0)[None, :]
     later_delta = jnp.sum(
         (later_d.astype(F32) * later_qo[:, share:].astype(F32)).reshape(window, heads, size),
         axis=2,
@@ -316,7 +498,7 @@
         functools.partial(key_kernel, **shape),
         jax.ShapeDtypeStruct((tokens, 2 * share), BF),
         (
-            jnp.stack([last_start, group * tokens]),
+            jnp.stack([group * tokens, group * tokens]),
             later_qo,
             later_d,
             pair,
@@ -365,34 +547,35 @@
     d_cols = both.reshape(2, tokens, 3, share).transpose(1, 2, 0, 3).reshape(tokens, 3 * half)
     g_in = mm_tn(cut(h_first, col, half, 1), d_cols).astype(BF)
     g_out = mm_tn(mixed_half, cut(d_branch, row, half, 1)).astype(BF)
-    g_in, g_out, g_down, g_up = lax.optimization_barrier((g_in, g_out, g_down, g_up))
-    g_in, g_out = lax.psum((g_in, g_out), "dp")
-
-    def spread(piece, extent):
-        whole = jnp.zeros((extent,), F32)
-        return lax.dynamic_update_slice_in_dim(whole, piece, place * piece.shape[0], 0)
 
     def total(array):
         return jnp.sum(array, axis=0, dtype=F32)
 
-    ours = 0.25
-    small = jnp.concatenate(
-        [
-            spread(total(d_query), model),
-            spread(total(d_values), model),
-            total(d_branch) * ours,
-            spread(total(d_share * n_share), model),
-            spread(total(d_share), model),
-            total(d_second * n_second) * ours,
-            total(d_second) * ours,
-            spread(total(d_gate), up_bias.shape[0]),
-            total(grad_full) * ours,
-        ]
-    )
-    small = lax.psum(small, ("dp",) + GRID)
-    parts = [small[at * model : (at + 1) * model] for at in range(7)]
-    g_up_bias = small[7 * model : 7 * model + up_bias.shape[0]]
-    g_down_bias = small[7 * model + up_bias.shape[0] :]
+    def own(vector):
+        return cut(vector, place, vector.shape[0] // 4, 0)
+
+    quarters = [
+        total(d_query),
+        total(d_values),
+        own(total(d_branch)),
+        own(total(d_second * n_second)),
+        own(total(d_second)),
+        own(total(grad_full)),
+        total(d_gate),
+    ]
+    sums = [total(d_first * n_first), total(d_first)]
+    lanes = 128
+    quarter_size = 6 * share + hidden_share
+    padding = jnp.zeros((40 * lanes - quarter_size - 2 * model,), F32)
+    small = jnp.concatenate(quarters + sums + [padding]).reshape(40, lanes)
+    grads, small = group_sum(jnp.concatenate([g_in, g_out], axis=1), small, groups)
+    g_in, g_out = grads[:, : 3 * half], grads[:, 3 * half :]
+    small = small.reshape(4, 40 * lanes)
+    wholes = [small[:, at * share : (at + 1) * share].reshape(model) for at in range(6)]
+    g_up_bias = small[:, 6 * share : quarter_size].reshape(4 * hidden_share)
+    g_down_bias = wholes[5]
+    firsts = jnp.sum(small[:, quarter_size : quarter_size + 2 * model], axis=0)
+    parts = wholes[:3] + [firsts[:model], firsts[model:]] + wholes[3:5]
     return (
         block_out,
         grad_in,

time: 573 us -> 440 us (0.77)
  waiting for transfers between devices: 343 us -> 130 us
  Pallas kernels: 19.8 us -> 139 us
  blocking collectives: 83 us -> 16.8 us
  starting transfers between devices: 20 us -> 48.8 us
    psum x3 -> x0, waiting for transfers between devices: 130 us -> none  [the longest x1 78 us: shards(): g_in, g_out = lax.psum((g_in, g_out), 'dp')]
    pallas_call x0 -> x3, Pallas kernels: none -> 120 us  [the longest x1 88.8 us: group_sum(): pl.pallas_call(functools.partial(group_sum_kernel, groups), out_shape=(ja...]
    ppermute x0 -> x16, waiting for transfers between devices: none -> 83.8 us  [from_behind(): lax.ppermute(array, 'dp', [(i, i + by) for i in range(groups) if 0 <= i +...]
    all_gather x3 -> x0, waiting for transfers between devices: 72.4 us -> none  [the longest x1 39.1 us: shards(): all_pairs = lax.all_gather(pair, 'dp', axis=0, tiled=True)]
    psum x1, waiting for transfers between devices: 84.1 us -> 42.5 us  [shards(): g_down, g_up = lax.psum((g_down, g_up), 'dp')]
    psum x1 -> x0, blocking collectives: 39.7 us -> none  [shards(): small = lax.psum(small, ('dp',) + GRID)]
    all_gather x1 -> x0, blocking collectives: 31.5 us -> none  [shards(): all_logs = lax.all_gather(log_total, 'dp', axis=0, tiled=True)]
    ppermute x0 -> x16, starting transfers between devices: none -> 28.5 us  [from_behind(): lax.ppermute(array, 'dp', [(i, i + by) for i in range(groups) if 0 <= i +...]
  transfers between devices with their start and end apart: 18 -> 28, of which waited for: 13 -> 9; matrix products, arithmetic and copies ran while one was open for 12% -> 16% of each run, Pallas kernels for 3% -> 30%
where the time goes in v2:
time: 440 us; the launch traced here: 437 us
  Pallas kernels  139 us (32%)
  waiting for transfers between devices  130 us (30%)
  starting transfers between devices  48.8 us (11%)
  local copies, waits for them, and re-layouts  37.5 us (9%)
  other arithmetic  30.9 us (7%)
  matrix products  17.3 us (4%)
  blocking collectives  16.8 us (4%)
  between operations  16.6 us (4%)
    pallas_call x1, Pallas kernels, group_sum(): pl.pallas_call(functools.partial(group_sum_kernel, groups), out_shape=(ja...  88.8 us
    ppermute x16, waiting for transfers between devices, from_behind(): lax.ppermute(array, 'dp', [(i, i + by) for i in range(groups) if 0 <= i +...  83.8 us
    psum x1, waiting for transfers between devices, shards(): g_down, g_up = lax.psum((g_down, g_up), 'dp')  42.5 us
    pallas_call x2, Pallas kernels, grid_sum(): pl.pallas_call(grid_sum_kernel, out_shape=jax.ShapeDtypeStruct((rows, col...  31.3 us
    ppermute x16, starting transfers between devices, from_behind(): lax.ppermute(array, 'dp', [(i, i + by) for i in range(groups) if 0 <= i +...  28.5 us
    pallas_call x3, Pallas kernels, local_kernel(): pl.pallas_call(body, out_shape=out_shape, in_specs=[pl.BlockSpec(memory_s...  19.3 us
    all_gather x1, blocking collectives, shards(): grad_full = lax.all_gather(grad_out, GRID, axis=1, tiled=True)  14.1 us
    unnamed x118, local copies, waits for them, and re-layouts  12.5 us
  transfers between devices with their start and end apart: 28, of which 9 were waited for; matrix products, arithmetic and copies ran while one was open for 16% of the time, Pallas kernels for 30%

profile of v2, /device:TPU:0, one launch (start us, length us, event | category | flops | bytes accessed | tf_op | source)
XLA Modules:
  0.0 437.1 jit_solution(10286358137445472204)
XLA Ops:
  9.2 3.0 collective-permute-start
  16.7 7.4 %collective-permute-start.6 = (bf16[960,384]{1,0:T(8,128)(2,1)}, bf16[960,384]{1,0:T(8,128)(2,1)}, u32[]{:S(2)}, u32[]{:S(2)}) collective-permute-start(bf16[960,384]{1,0:T(8,128)(2,1)} %pad_maximum_fusion.7), channel_id=1, source_target_pairs={{0,0},{1,2},{2,1},{3,3},{4,4},{5,6},{6,5},{7,7},{8,8},{9,10},{10,9... | collective-permute-start | bytes 2211848 | tf_op jit(solution)/shard_map/ppermute | solution.py:387
  25.0 14.1 %all_gather.12 = bf16[384,768]{0,1:T(8,128)(2,1)S(1)} all-gather(bf16[384,192]{0,1:T(8,128)(2,1)S(1)} %copy-done.41), channel_id=1, replica_groups=mesh['dp'=8,'row'=2,'col'=2] {'row','col'}, dimensions={1}, use_global_device_ids=true | all-gather | bytes 737280 | tf_op jit(solution)/shard_map/all_gather | solution.py:393
  52.5 3.7 collective-permute-start.4
  56.3 4.4 %collective-permute-start.3 = (bf16[384,384]{1,0:T(8,128)(2,1)S(1)}, bf16[384,384]{1,0:T(8,128)(2,1)S(1)}, u32[]{:S(2)}, u32[]{:S(2)}) collective-permute-start(bf16[384,384]{1,0:T(8,128)(2,1)S(1)} %slice.137.kv_ref), channel_id=1, source_target_pairs={{0,12},{4,16},{8,20},{12,24},{16,28},{1,13},{5,17},{9,21},{13,25},... | collective-permute-start | bytes 884744 | tf_op jit(solution)/shard_map/ppermute | solution.py:322
  68.0 7.7 %collective-permute-done.2 = bf16[384,384]{1,0:T(8,128)(2,1)S(1)} collective-permute-done((bf16[384,384]{1,0:T(8,128)(2,1)S(1)}, bf16[384,384]{1,0:T(8,128)(2,1)S(1)}, u32[]{:S(2)}, u32[]{:S(2)}) %collective-permute-start.2) | collective-permute-done | bytes 294944 | tf_op jit(solution)/shard_map/ppermute | solution.py:322
  76.2 6.2 %shard_map.271 = (bf16[384,192]{1,0:T(8,128)(2,1)S(1)}, f32[384,3]{1,0:T(8,128)S(1)}) custom-call(s32[2]{0:T(128)S(1)} %pad_add_fusion.base_ref, bf16[384,192]{1,0:T(8,128)(2,1)S(1)} %slice.136.q_ref, bf16[1920,384]{1,0:T(8,128)(2,1)S(1)} %constant_dynamic-update-slice_fusion.kv_ref, s32[384,1]{1,0:T(8,128)S(1)} %broadcast_in_dim.32.start_ref), custom_call_target="tpu_custom_call" | custom-call | flops 566231040 | bytes 8388608 | tf_op jit(solution)/shard_map/pallas_call | solution.py:138
  88.2 14.8 %shard_map.272 = bf16[384,768]{1,0:T(8,128)(2,1)S(1)} custom-call(bf16[384,768]{1,0:T(8,128)(2,1)S(1)} %convolution_convert_fusion.5.source), custom_call_target="tpu_custom_call" | custom-call | flops 1179648 | bytes 25165824 | tf_op jit(solution)/shard_map/pallas_call | solution.py:217
  111.2 16.5 %shard_map.273 = bf16[384,768]{1,0:T(8,128)(2,1)S(1)} custom-call(bf16[384,768]{1,0:T(8,128)(2,1)S(1)} %convolution_convert_fusion.3.source), custom_call_target="tpu_custom_call" | custom-call | flops 1179648 | bytes 25165824 | tf_op jit(solution)/shard_map/pallas_call | solution.py:217
  137.6 3.1 fusion.6
  143.1 6.1 %shard_map.274 = bf16[384,192]{1,0:T(8,128)(2,1)S(1)} custom-call(s32[2]{0:T(128)S(1)} %pad_add_fusion.base_ref, bf16[384,192]{1,0:T(8,128)(2,1)S(1)} %slice.136.q_ref, bf16[1920,384]{1,0:T(8,128)(2,1)S(1)} %copy-done.8, s32[384,1]{1,0:T(8,128)S(1)} %copy-done.3, f32[384,3]{1,0:T(8,128)S(1)} %copy-done.5, f32[384,3]{1,0:T(8,128)S(1)} %copy-done.6, ...), custom_call_target="tpu_custom_call" | custom-call | flops 849346560 | bytes 8388608 | tf_op jit(solution)/shard_map/pallas_call | solution.py:138
  149.2 7.3 %collective-permute-start.22 = (bf16[384,960]{0,1:T(8,128)(2,1)}, bf16[384,960]{0,1:T(8,128)(2,1)}, u32[]{:S(2)}, u32[]{:S(2)}) collective-permute-start(bf16[384,960]{0,1:T(8,128)(2,1)} %copy.106), channel_id=1, source_target_pairs={{0,0},{1,2},{2,1},{3,3},{4,4},{5,6},{6,5},{7,7},{8,8},{9,10},{10,9... | collective-permute-start | bytes 2211848 | tf_op jit(solution)/shard_map/ppermute | solution.py:459
  161.2 11.2 %collective-permute-done.13 = bf16[384,192]{1,0:T(8,128)(2,1)S(1)} collective-permute-done((bf16[384,192]{1,0:T(8,128)(2,1)S(1)}, bf16[384,192]{1,0:T(8,128)(2,1)S(1)}, u32[]{:S(2)}, u32[]{:S(2)}) %collective-permute-start.13) | collective-permute-done | bytes 147488 | tf_op jit(solution)/shard_map/ppermute | solution.py:322
  173.8 3.2 collective-permute-done.14
  178.3 24.3 %collective-permute-done.15 = bf16[384,192]{1,0:T(8,128)(2,1)S(1)} collective-permute-done((bf16[384,192]{1,0:T(8,128)(2,1)S(1)}, bf16[384,192]{1,0:T(8,128)(2,1)S(1)}, u32[]{:S(2)}, u32[]{:S(2)}) %collective-permute-start.15) | collective-permute-done | bytes 147488 | tf_op jit(solution)/shard_map/ppermute | solution.py:322
  206.6 8.5 %collective-permute-done.10 = bf16[384,384]{1,0:T(8,128)(2,1)S(1)} collective-permute-done((bf16[384,384]{1,0:T(8,128)(2,1)}, bf16[384,384]{1,0:T(8,128)(2,1)S(1)}, u32[]{:S(2)}, u32[]{:S(2)}) %collective-permute-start.10) | collective-permute-done | bytes 294944 | tf_op jit(solution)/shard_map/ppermute | solution.py:322
  215.2 7.9 %collective-permute-done.11 = bf16[384,384]{1,0:T(8,128)(2,1)S(1)} collective-permute-done((bf16[384,384]{1,0:T(8,128)(2,1)}, bf16[384,384]{1,0:T(8,128)(2,1)S(1)}, u32[]{:S(2)}, u32[]{:S(2)}) %collective-permute-start.11) | collective-permute-done | bytes 294944 | tf_op jit(solution)/shard_map/ppermute | solution.py:322
  223.1 20.9 %collective-permute-done.12 = bf16[384,384]{1,0:T(8,128)(2,1)S(1)} collective-permute-done((bf16[384,384]{1,0:T(8,128)(2,1)}, bf16[384,384]{1,0:T(8,128)(2,1)S(1)}, u32[]{:S(2)}, u32[]{:S(2)}) %collective-permute-start.12) | collective-permute-done | bytes 294944 | tf_op jit(solution)/shard_map/ppermute | solution.py:322
  250.1 7.0 %shard_map.275 = bf16[384,384]{1,0:T(8,128)(2,1)S(1)} custom-call(s32[2]{0:T(128)S(1)} %pad_add_fusion.1.base_ref, bf16[1920,384]{1,0:T(8,128)(2,1)S(1)} %constant_dynamic-update-slice_fusion.5.qo_ref, bf16[1920,192]{1,0:T(8,128)(2,1)S(1)} %constant_dynamic-update-slice_fusion.10.do_ref, bf16[384,384]{1,0:T(8,128)(2,1)S(1)} %copy-done.1, ...), custom_call_target="tpu_custom_call" | custom-call | flops 1132462080 | bytes 8388608 | tf_op jit(solution)/shard_map/pallas_call | solution.py:138
  261.4 3.2 collective-permute-done.21
  274.6 3.1 convolution_convert_fusion.2
  279.2 88.8 %shard_map.276 = (bf16[384,1536]{1,0:T(8,128)(2,1)S(1)}, f32[4,40,128]{2,1,0:T(8,128)S(1)}) custom-call(bf16[384,1536]{1,0:T(8,128)(2,1)S(1)} %pad_maximum_fusion.2.source, f32[40,128]{1,0:T(8,128)S(1)} %bitcast.37), custom_call_target="tpu_custom_call" | custom-call | flops 4718592 | bytes 104857600 | tf_op jit(solution)/shard_map/pallas_call | solution.py:297
  382.5 42.5 %all-reduce.4.cloned.1.call-done = (bf16[384,1536]{1,0:T(8,128)(2,1)}, bf16[1536,384]{1,0:T(8,128)(2,1)}) async-done(((bf16[384,1536]{1,0:T(8,128)(2,1)}, bf16[1536,384]{1,0:T(8,128)(2,1)}), (bf16[384,1536]{1,0:T(8,128)(2,1)}, bf16[1536,384]{1,0:T(8,128)(2,1)})) %all-reduce.4.cloned.1.call-update) | async-done | bytes 2359312 | tf_op jit(solution)/shard_map/psum | solution.py:469
  425.0 3.1 convert_element_type.131
  (278 shorter events, 102.2 us)
Async XLA Ops:
  8.0 266.5 %all-gather.3.cloned.1.call-start = ((), (), s32[]{:S(2)}) async-start(), calls=%async_computation.3 | async-start | bytes 1769472 | tf_op jit(solution)/shard_map/all_gather | solution.py:465
  9.2 36.9 %collective-permute-start = (bf16[384,384]{1,0:T(8,128)(2,1)S(1)}, bf16[384,384]{1,0:T(8,128)(2,1)}, u32[]{:S(2)}, u32[]{:S(2)}) collective-permute-start(bf16[384,384]{1,0:T(8,128)(2,1)S(1)} %slice.104), channel_id=1, source_target_pairs={{0,2},{2,0},{1,3},{3,1},{4,6},{6,4},{5,7},{7,5},{8,10},{10,8},{9,1... | collective-permute-start | bytes 884744 | tf_op jit(solution)/shard_map/ppermute | solution.py:361
  14.1 34.5 %collective-permute-start.8 = (bf16[384,768]{1,0:T(8,128)(2,1)}, bf16[384,768]{1,0:T(8,128)(2,1)}, u32[]{:S(2)}, u32[]{:S(2)}) collective-permute-start(bf16[384,768]{1,0:T(8,128)(2,1)} %constant_dynamic-slice_fusion), channel_id=1, source_target_pairs={{0,1},{1,0},{2,3},{3,2},{4,5},{5,4},{6,7},{7,6},{8,9},{9,8},{10,11... | collective-permute-start | bytes 1769480 | tf_op jit(solution)/shard_map/ppermute | solution.py:377
  15.3 47.7 %collective-permute-start.7 = (bf16[960,384]{1,0:T(8,128)(2,1)}, bf16[960,384]{1,0:T(8,128)(2,1)}, u32[]{:S(2)}, u32[]{:S(2)}) collective-permute-start(bf16[960,384]{1,0:T(8,128)(2,1)} %pad_maximum_fusion.8), channel_id=1, source_target_pairs={{0,1},{1,3},{2,0},{3,2},{4,5},{5,7},{6,4},{7,6},{8,9},{9,11},{10,8... | collective-permute-start | bytes 2211848 | tf_op jit(solution)/shard_map/ppermute | solution.py:388
  16.7 46.3 %collective-permute-start.6 = (bf16[960,384]{1,0:T(8,128)(2,1)}, bf16[960,384]{1,0:T(8,128)(2,1)}, u32[]{:S(2)}, u32[]{:S(2)}) collective-permute-start(bf16[960,384]{1,0:T(8,128)(2,1)} %pad_maximum_fusion.7), channel_id=1, source_target_pairs={{0,0},{1,2},{2,1},{3,3},{4,4},{5,6},{6,5},{7,7},{8,8},{9,10},{10,9... | collective-permute-start | bytes 2211848 | tf_op jit(solution)/shard_map/ppermute | solution.py:387
  52.5 23.3 %collective-permute-start.4 = (bf16[384,384]{1,0:T(8,128)(2,1)S(1)}, bf16[384,384]{1,0:T(8,128)(2,1)S(1)}, u32[]{:S(2)}, u32[]{:S(2)}) collective-permute-start(bf16[384,384]{1,0:T(8,128)(2,1)S(1)} %slice.137.kv_ref), channel_id=1, source_target_pairs={{0,8},{4,12},{8,16},{12,20},{16,24},{20,28},{1,9},{5,13},{9,17},{1... | collective-permute-start | bytes 884744 | tf_op jit(solution)/shard_map/ppermute | solution.py:322
  56.3 19.5 %collective-permute-start.3 = (bf16[384,384]{1,0:T(8,128)(2,1)S(1)}, bf16[384,384]{1,0:T(8,128)(2,1)S(1)}, u32[]{:S(2)}, u32[]{:S(2)}) collective-permute-start(bf16[384,384]{1,0:T(8,128)(2,1)S(1)} %slice.137.kv_ref), channel_id=1, source_target_pairs={{0,12},{4,16},{8,20},{12,24},{16,28},{1,13},{5,17},{9,21},{13,25},... | collective-permute-start | bytes 884744 | tf_op jit(solution)/shard_map/ppermute | solution.py:322
  60.7 15.1 %collective-permute-start.2 = (bf16[384,384]{1,0:T(8,128)(2,1)S(1)}, bf16[384,384]{1,0:T(8,128)(2,1)S(1)}, u32[]{:S(2)}, u32[]{:S(2)}) collective-permute-start(bf16[384,384]{1,0:T(8,128)(2,1)S(1)} %slice.137.kv_ref), channel_id=1, source_target_pairs={{0,16},{4,20},{8,24},{12,28},{1,17},{5,21},{9,25},{13,29},{2,18},{... | collective-permute-start | bytes 884744 | tf_op jit(solution)/shard_map/ppermute | solution.py:322
  82.5 77.4 %collective-permute-start.20 = (f32[3,384]{1,0:T(4,128)S(1)}, f32[3,384]{1,0:T(4,128)S(1)}, u32[]{:S(2)}, u32[]{:S(2)}) collective-permute-start(f32[3,384]{1,0:T(4,128)S(1)} %bitcast.47), channel_id=1, source_target_pairs={{16,0},{20,4},{24,8},{28,12},{17,1},{21,5},{25,9},{29,13},{18,2},{... | collective-permute-start | bytes 13832 | tf_op jit(solution)/shard_map/ppermute | solution.py:322
  84.0 74.6 %collective-permute-start.19 = (f32[3,384]{1,0:T(4,128)S(1)}, f32[3,384]{1,0:T(4,128)S(1)}, u32[]{:S(2)}, u32[]{:S(2)}) collective-permute-start(f32[3,384]{1,0:T(4,128)S(1)} %bitcast.48), channel_id=1, source_target_pairs={{12,0},{16,4},{20,8},{24,12},{28,16},{13,1},{17,5},{21,9},{25,13},... | collective-permute-start | bytes 13832 | tf_op jit(solution)/shard_map/ppermute | solution.py:322
  85.3 72.0 %collective-permute-start.18 = (f32[3,384]{1,0:T(4,128)S(1)}, f32[3,384]{1,0:T(4,128)S(1)}, u32[]{:S(2)}, u32[]{:S(2)}) collective-permute-start(f32[3,384]{1,0:T(4,128)S(1)} %bitcast.49), channel_id=1, source_target_pairs={{8,0},{12,4},{16,8},{20,12},{24,16},{28,20},{9,1},{13,5},{17,9},{2... | collective-permute-start | bytes 13832 | tf_op jit(solution)/shard_map/ppermute | solution.py:322
  86.6 62.6 %collective-permute-start.17 = (f32[3,384]{1,0:T(4,128)S(1)}, f32[3,384]{1,0:T(4,128)}, u32[]{:S(2)}, u32[]{:S(2)}) collective-permute-start(f32[3,384]{1,0:T(4,128)S(1)} %bitcast.50), channel_id=1, source_target_pairs={{4,0},{8,4},{12,8},{16,12},{20,16},{24,20},{28,24},{5,1},{9,5},{13... | collective-permute-start | bytes 13832 | tf_op jit(solution)/shard_map/ppermute | solution.py:322
  111.0 264.5 %reduce-scatter.7.cloned.1.call-start = ((), (), s32[]{:S(2)}) async-start(), calls=%async_computation.4 | async-start | bytes 737280
  132.1 137.9 %collective-permute-start.23 = (bf16[384,960]{0,1:T(8,128)(2,1)}, bf16[384,960]{0,1:T(8,128)(2,1)}, u32[]{:S(2)}, u32[]{:S(2)}) collective-permute-start(bf16[384,960]{0,1:T(8,128)(2,1)} %copy.106), channel_id=1, source_target_pairs={{0,2},{1,0},{2,3},{3,1},{4,6},{5,4},{6,7},{7,5},{8,10},{9,8},{10,1... | collective-permute-start | bytes 2211848 | tf_op jit(solution)/shard_map/ppermute | solution.py:460
  149.2 229.6 %reduce-scatter.5.cloned.1.call-start = ((), (), s32[]{:S(2)}) async-start(), calls=%async_computation.2 | async-start | bytes 983040 | tf_op jit(solution)/shard_map/reduce_scatter | solution.py:532
  149.2 120.9 %collective-permute-start.22 = (bf16[384,960]{0,1:T(8,128)(2,1)}, bf16[384,960]{0,1:T(8,128)(2,1)}, u32[]{:S(2)}, u32[]{:S(2)}) collective-permute-start(bf16[384,960]{0,1:T(8,128)(2,1)} %copy.106), channel_id=1, source_target_pairs={{0,0},{1,2},{2,1},{3,3},{4,4},{5,6},{6,5},{7,7},{8,8},{9,10},{10,9... | collective-permute-start | bytes 2211848 | tf_op jit(solution)/shard_map/ppermute | solution.py:459
  157.3 46.7 %collective-permute-start.16 = (bf16[384,192]{1,0:T(8,128)(2,1)S(1)}, bf16[384,192]{1,0:T(8,128)(2,1)S(1)}, u32[]{:S(2)}, u32[]{:S(2)}) collective-permute-start(bf16[384,192]{1,0:T(8,128)(2,1)S(1)} %get-tuple-element.143.do_ref), channel_id=1, source_target_pairs={{16,0},{20,4},{24,8},{28,12},{17,1},{21,5},{25,9},{29,13},{18,2},{... | collective-permute-start | bytes 442376 | tf_op jit(solution)/shard_map/ppermute | solution.py:322
  158.6 13.9 %collective-permute-start.13 = (bf16[384,192]{1,0:T(8,128)(2,1)S(1)}, bf16[384,192]{1,0:T(8,128)(2,1)S(1)}, u32[]{:S(2)}, u32[]{:S(2)}) collective-permute-start(bf16[384,192]{1,0:T(8,128)(2,1)S(1)} %get-tuple-element.143.do_ref), channel_id=1, source_target_pairs={{4,0},{8,4},{12,8},{16,12},{20,16},{24,20},{28,24},{5,1},{9,5},{13... | collective-permute-start | bytes 442376 | tf_op jit(solution)/shard_map/ppermute | solution.py:322
  159.9 17.1 %collective-permute-start.14 = (bf16[384,192]{1,0:T(8,128)(2,1)S(1)}, bf16[384,192]{1,0:T(8,128)(2,1)S(1)}, u32[]{:S(2)}, u32[]{:S(2)}) collective-permute-start(bf16[384,192]{1,0:T(8,128)(2,1)S(1)} %get-tuple-element.143.do_ref), channel_id=1, source_target_pairs={{8,0},{12,4},{16,8},{20,12},{24,16},{28,20},{9,1},{13,5},{17,9},{2... | collective-permute-start | bytes 442376 | tf_op jit(solution)/shard_map/ppermute | solution.py:322
  172.4 30.2 %collective-permute-start.15 = (bf16[384,192]{1,0:T(8,128)(2,1)S(1)}, bf16[384,192]{1,0:T(8,128)(2,1)S(1)}, u32[]{:S(2)}, u32[]{:S(2)}) collective-permute-start(bf16[384,192]{1,0:T(8,128)(2,1)S(1)} %get-tuple-element.143.do_ref), channel_id=1, source_target_pairs={{12,0},{16,4},{20,8},{24,12},{28,16},{13,1},{17,5},{21,9},{25,13},... | collective-permute-start | bytes 442376 | tf_op jit(solution)/shard_map/ppermute | solution.py:322
  177.0 28.3 %collective-permute-start.9 = (bf16[384,384]{1,0:T(8,128)(2,1)}, bf16[384,384]{1,0:T(8,128)(2,1)S(1)}, u32[]{:S(2)}, u32[]{:S(2)}) collective-permute-start(bf16[384,384]{1,0:T(8,128)(2,1)} %get-tuple-element.99), channel_id=1, source_target_pairs={{4,0},{8,4},{12,8},{16,12},{20,16},{24,20},{28,24},{5,1},{9,5},{13... | collective-permute-start | bytes 884744 | tf_op jit(solution)/shard_map/ppermute | solution.py:322
  203.9 19.1 %collective-permute-start.11 = (bf16[384,384]{1,0:T(8,128)(2,1)}, bf16[384,384]{1,0:T(8,128)(2,1)S(1)}, u32[]{:S(2)}, u32[]{:S(2)}) collective-permute-start(bf16[384,384]{1,0:T(8,128)(2,1)} %get-tuple-element.99), channel_id=1, source_target_pairs={{12,0},{16,4},{20,8},{24,12},{28,16},{13,1},{17,5},{21,9},{25,13},... | collective-permute-start | bytes 884744 | tf_op jit(solution)/shard_map/ppermute | solution.py:322
  205.3 38.7 %collective-permute-start.12 = (bf16[384,384]{1,0:T(8,128)(2,1)}, bf16[384,384]{1,0:T(8,128)(2,1)S(1)}, u32[]{:S(2)}, u32[]{:S(2)}) collective-permute-start(bf16[384,384]{1,0:T(8,128)(2,1)} %get-tuple-element.99), channel_id=1, source_target_pairs={{16,0},{20,4},{24,8},{28,12},{17,1},{21,5},{25,9},{29,13},{18,2},{... | collective-permute-start | bytes 884744 | tf_op jit(solution)/shard_map/ppermute | solution.py:322
  260.7 164.3 %all-reduce.4.cloned.1.call-start = ((), (), s32[]{:S(2)}) async-start(), calls=%async_computation.5 | async-start | bytes 4718592 | tf_op jit(solution)/shard_map/psum | solution.py:469
  (54 other events, 347.0 us)
Sparse Core Ops, SparseCore 0:
  111.1 35.5 all-gather.2
  277.8 147.1 all-reduce.3
Sparse Core Ops, SparseCore 1:
  149.2 47.7 reduce-scatter.6
  260.8 20.9 reduce-scatter.4

commit v3 on v2

--- a/solution.py
+++ b/solution.py
@@ -390,7 +390,6 @@
         [jnp.where(left, part_a, part_b), jnp.where(left, part_b, part_a)], axis=1
     )
     out_own, down_own = rows_own[:share], rows_own[share:]
-    grad_full = lax.all_gather(grad_out, GRID, axis=1, tiled=True)
 
     bounds = jnp.cumsum(lengths)
     everywhere = jnp.arange(tokens * groups, dtype=jnp.int32)
@@ -411,6 +410,8 @@
     )
     qkv = (mm(h_first, in_own) + bias_own).astype(BF)
     queries, pair = qkv[:, :share], qkv[:, share:]
+    pair, grad_out = lax.optimization_barrier((pair, grad_out))
+    grad_full = lax.all_gather(grad_out, GRID, axis=1, tiled=True)
     pairs = jnp.concatenate(
         [from_behind(pair, by, groups) for by in range(visits, 0, -1)] + [pair], axis=0
     )
@@ -458,6 +459,9 @@
     acts = jnp.concatenate([hidden, mixed], axis=1)
     acts_a = lax.ppermute(acts, GRID, TRANSPOSE)
     acts_b = lax.ppermute(acts, GRID, FROM_FLIPPED)
+    d_second, later_qo, later_log, acts_a, acts_b = lax.optimization_barrier(
+        (d_second, later_qo, later_log, acts_a, acts_b)
+    )
     acts_0 = jnp.where(top, acts_a, acts_b)
     acts_1 = jnp.where(top, acts_b, acts_a)
     hidden_half = jnp.concatenate([acts_0[:, :hidden_share], acts_1[:, :hidden_share]], axis=1)
@@ -466,6 +470,7 @@
 
     g_down = mm_tn(hidden_half, cut(grad_full, row, half, 1)).astype(BF)
     g_up = mm_tn(cut(h_second, col, half, 1), d_gate_half).astype(BF)
+    d_second, g_down, g_up = lax.optimization_barrier((d_second, g_down, g_up))
     g_down, g_up = lax.psum((g_down, g_up), "dp")
 
     e_second = d_second * gain_second
@@ -508,6 +513,7 @@
         ),
         8 * tokens * window * share,
     )
+    d_pair, d_query, g_down, g_up = lax.optimization_barrier((d_pair, d_query, g_down, g_up))
     d_keys, d_values = d_pair[:, :share], d_pair[:, share:]
     d_qkv = jnp.concatenate([d_query, d_pair], axis=1)
 

time: 440 us -> 413 us (0.939)
  Pallas kernels: 139 us -> 107 us
  blocking collectives: 16.8 us -> 9.46 us
  waiting for transfers between devices: 130 us -> 136 us
  starting transfers between devices: 48.8 us -> 43.3 us
    pallas_call x1, Pallas kernels: 88.8 us -> 55 us  [group_sum(): pl.pallas_call(functools.partial(group_sum_kernel, groups), out_shape=(ja...]
    psum x1, waiting for transfers between devices: 42.5 us -> 67.5 us  [shards(): g_down, g_up = lax.psum((g_down, g_up), 'dp')]
    ppermute x16, waiting for transfers between devices: 83.8 us -> 68 us  [from_behind(): lax.ppermute(array, 'dp', [(i, i + by) for i in range(groups) if 0 <= i +...]
    all_gather x1, blocking collectives: 14.1 us -> 6.74 us  [shards(): grad_full = lax.all_gather(grad_out, GRID, axis=1, tiled=True)]
    ppermute x1, starting transfers between devices: 7.35 us -> 1.77 us  [shards(): acts_a = lax.ppermute(acts, GRID, TRANSPOSE)]
    unnamed x118 -> x100, local copies, waits for them, and re-layouts: 12.5 us -> 13 us
  transfers between devices with their start and end apart: 28 -> 28, of which waited for: 9 -> 8; matrix products, arithmetic and copies ran while one was open for 16% -> 19% of each run, Pallas kernels for 30% -> 21%
where the time goes in v3:
time: 413 us; the launch traced here: 407 us
  waiting for transfers between devices  136 us (33%)
  Pallas kernels  107 us (26%)
  starting transfers between devices  43.3 us (10%)
  local copies, waits for them, and re-layouts  41.8 us (10%)
  other arithmetic  35 us (8%)
  matrix products  18.7 us (5%)
  between operations  16.5 us (4%)
  blocking collectives  9.46 us (2%)
    ppermute x16, waiting for transfers between devices, from_behind(): lax.ppermute(array, 'dp', [(i, i + by) for i in range(groups) if 0 <= i +...  68 us
    psum x1, waiting for transfers between devices, shards(): g_down, g_up = lax.psum((g_down, g_up), 'dp')  67.5 us
    pallas_call x1, Pallas kernels, group_sum(): pl.pallas_call(functools.partial(group_sum_kernel, groups), out_shape=(ja...  55 us
    pallas_call x2, Pallas kernels, grid_sum(): pl.pallas_call(grid_sum_kernel, out_shape=jax.ShapeDtypeStruct((rows, col...  31.9 us
    ppermute x16, starting transfers between devices, from_behind(): lax.ppermute(array, 'dp', [(i, i + by) for i in range(groups) if 0 <= i +...  28.9 us
    pallas_call x3, Pallas kernels, local_kernel(): pl.pallas_call(body, out_shape=out_shape, in_specs=[pl.BlockSpec(memory_s...  19.9 us
    unnamed x100, local copies, waits for them, and re-layouts  13 us
  transfers between devices with their start and end apart: 28, of which 8 were waited for; matrix products, arithmetic and copies ran while one was open for 19% of the time, Pallas kernels for 21%

profile of v3, /device:TPU:0, one launch (start us, length us, event | category | flops | bytes accessed | tf_op | source)
XLA Modules:
  0.0 407.1 jit_solution(2851932035656391246)
XLA Ops:
  9.2 3.0 collective-permute-start
  15.9 7.3 %collective-permute-start.6 = (bf16[960,384]{1,0:T(8,128)(2,1)}, bf16[960,384]{1,0:T(8,128)(2,1)}, u32[]{:S(2)}, u32[]{:S(2)}) collective-permute-start(bf16[960,384]{1,0:T(8,128)(2,1)} %pad_maximum_fusion.7), channel_id=1, source_target_pairs={{0,0},{1,2},{2,1},{3,3},{4,4},{5,6},{6,5},{7,7},{8,8},{9,10},{10,9... | collective-permute-start | bytes 2211848 | tf_op jit(solution)/shard_map/ppermute | solution.py:387
  34.1 3.6 collective-permute-start.4
  37.8 4.4 %collective-permute-start.3 = (bf16[384,384]{1,0:T(8,128)(2,1)S(1)}, bf16[384,384]{1,0:T(8,128)(2,1)S(1)}, u32[]{:S(2)}, u32[]{:S(2)}) collective-permute-start(bf16[384,384]{1,0:T(8,128)(2,1)S(1)} %slice.137.kv_ref), channel_id=1, source_target_pairs={{0,12},{4,16},{8,20},{12,24},{16,28},{1,13},{5,17},{9,21},{13,25},... | collective-permute-start | bytes 884744 | tf_op jit(solution)/shard_map/ppermute | solution.py:322
  42.2 2.3 collective-permute-start.2
  45.8 6.7 %all_gather.12 = bf16[384,768]{0,1:T(8,128)(2,1)S(1)} all-gather(bf16[384,192]{0,1:T(8,128)(2,1)S(1)} %copy-done.34), channel_id=1, replica_groups=mesh['dp'=8,'row'=2,'col'=2] {'row','col'}, dimensions={1}, use_global_device_ids=true | all-gather | bytes 737280 | tf_op jit(solution)/shard_map/all_gather | solution.py:414
  52.6 2.5 collective-permute-start.5
  57.0 4.8 %collective-permute-done.5 = bf16[384,384]{1,0:T(8,128)(2,1)S(1)} collective-permute-done((bf16[384,384]{1,0:T(8,128)(2,1)S(1)}, bf16[384,384]{1,0:T(8,128)(2,1)S(1)}, u32[]{:S(2)}, u32[]{:S(2)}) %collective-permute-start.5) | collective-permute-done | bytes 294944 | tf_op jit(solution)/shard_map/ppermute | solution.py:322
  62.0 6.2 %shard_map.271 = (bf16[384,192]{1,0:T(8,128)(2,1)S(1)}, f32[384,3]{1,0:T(8,128)S(1)}) custom-call(s32[2]{0:T(128)S(1)} %pad_add_fusion.base_ref, bf16[384,192]{1,0:T(8,128)(2,1)S(1)} %slice.136.q_ref, bf16[1920,384]{1,0:T(8,128)(2,1)S(1)} %constant_dynamic-update-slice_fusion.kv_ref, s32[384,1]{1,0:T(8,128)S(1)} %broadcast_in_dim.32.start_ref), custom_call_target="tpu_custom_call" | custom-call | flops 566231040 | bytes 8388608 | tf_op jit(solution)/shard_map/pallas_call | solution.py:138
  68.6 15.5 %shard_map.272 = bf16[384,768]{1,0:T(8,128)(2,1)S(1)} custom-call(bf16[384,768]{1,0:T(8,128)(2,1)S(1)} %convolution_convert_fusion.5.source), custom_call_target="tpu_custom_call" | custom-call | flops 1179648 | bytes 25165824 | tf_op jit(solution)/shard_map/pallas_call | solution.py:217
  104.1 16.4 %shard_map.273 = bf16[384,768]{1,0:T(8,128)(2,1)S(1)} custom-call(bf16[384,768]{1,0:T(8,128)(2,1)S(1)} %convolution_convert_fusion.3.source), custom_call_target="tpu_custom_call" | custom-call | flops 1179648 | bytes 25165824 | tf_op jit(solution)/shard_map/pallas_call | solution.py:217
  127.5 8.4 %collective-permute-done.9 = bf16[384,384]{1,0:T(8,128)(2,1)S(1)} collective-permute-done((bf16[384,384]{1,0:T(8,128)(2,1)}, bf16[384,384]{1,0:T(8,128)(2,1)S(1)}, u32[]{:S(2)}, u32[]{:S(2)}) %collective-permute-start.9) | collective-permute-done | bytes 294944 | tf_op jit(solution)/shard_map/ppermute | solution.py:322
  137.2 8.8 %collective-permute-done.10 = bf16[384,384]{1,0:T(8,128)(2,1)S(1)} collective-permute-done((bf16[384,384]{1,0:T(8,128)(2,1)}, bf16[384,384]{1,0:T(8,128)(2,1)S(1)}, u32[]{:S(2)}, u32[]{:S(2)}) %collective-permute-start.10) | collective-permute-done | bytes 294944 | tf_op jit(solution)/shard_map/ppermute | solution.py:322
  146.1 14.3 %collective-permute-done.11 = bf16[384,384]{1,0:T(8,128)(2,1)S(1)} collective-permute-done((bf16[384,384]{1,0:T(8,128)(2,1)}, bf16[384,384]{1,0:T(8,128)(2,1)S(1)}, u32[]{:S(2)}, u32[]{:S(2)}) %collective-permute-start.11) | collective-permute-done | bytes 294944 | tf_op jit(solution)/shard_map/ppermute | solution.py:322
  160.5 25.2 %collective-permute-done.12 = bf16[384,384]{1,0:T(8,128)(2,1)S(1)} collective-permute-done((bf16[384,384]{1,0:T(8,128)(2,1)}, bf16[384,384]{1,0:T(8,128)(2,1)S(1)}, u32[]{:S(2)}, u32[]{:S(2)}) %collective-permute-start.12) | collective-permute-done | bytes 294944 | tf_op jit(solution)/shard_map/ppermute | solution.py:322
  191.5 3.2 convolution_convert_fusion.1
  198.0 3.3 convert_reduce_fusion.3
  220.1 6.6 %shard_map.275 = bf16[384,192]{1,0:T(8,128)(2,1)S(1)} custom-call(s32[2]{0:T(128)S(1)} %pad_add_fusion.base_ref, bf16[384,192]{1,0:T(8,128)(2,1)S(1)} %slice.136.q_ref, bf16[1920,384]{1,0:T(8,128)(2,1)S(1)} %copy-done.4, s32[384,1]{1,0:T(8,128)S(1)} %broadcast_in_dim.32.start_ref, f32[384,3]{1,0:T(8,128)S(1)} %copy-done.1, f32[384,3]{1,0:T(8,128)S(1)} %copy-done.2, ...), custom_call_target="tpu_custom_call" | custom-call | flops 849346560 | bytes 8388608 | tf_op jit(solution)/shard_map/pallas_call | solution.py:138
  229.9 4.7 %collective-permute-done.20 = bf16[384,192]{1,0:T(8,128)(2,1)} collective-permute-done((bf16[384,192]{1,0:T(8,128)(2,1)}, bf16[384,192]{1,0:T(8,128)(2,1)}, u32[]{:S(2)}, u32[]{:S(2)}) %collective-permute-start.20) | collective-permute-done | bytes 147488 | tf_op jit(solution)/shard_map/ppermute | solution.py:322
  239.1 2.7 copy.94
  243.4 7.0 %shard_map.274 = bf16[384,384]{1,0:T(8,128)(2,1)S(1)} custom-call(s32[2]{0:T(128)S(1)} %pad_add_fusion.1.base_ref, bf16[1920,384]{1,0:T(8,128)(2,1)S(1)} %constant_dynamic-update-slice_fusion.5.qo_ref, bf16[1920,192]{1,0:T(8,128)(2,1)S(1)} %constant_dynamic-update-slice_fusion.15.do_ref, bf16[384,384]{1,0:T(8,128)(2,1)S(1)} %slice.137.kv_ref, ...), custom_call_target="tpu_custom_call" | custom-call | flops 1132462080 | bytes 8388608 | tf_op jit(solution)/shard_map/pallas_call | solution.py:138
  250.4 67.5 %all-reduce.4.cloned.1.call-done = (bf16[1536,384]{1,0:T(8,128)(2,1)}, bf16[384,1536]{1,0:T(8,128)(2,1)}) async-done(((bf16[1536,384]{1,0:T(8,128)(2,1)}, bf16[384,1536]{1,0:T(8,128)(2,1)}), (bf16[1536,384]{1,0:T(8,128)(2,1)}, bf16[384,1536]{1,0:T(8,128)(2,1)})) %all-reduce.4.cloned.1.call-update) | async-done | bytes 2359312 | tf_op jit(solution)/shard_map/psum | solution.py:474
  328.0 2.7 all-gather
  333.4 55.0 %shard_map.276 = (bf16[384,1536]{1,0:T(8,128)(2,1)S(1)}, f32[4,40,128]{2,1,0:T(8,128)S(1)}) custom-call(bf16[384,1536]{1,0:T(8,128)(2,1)S(1)} %pad_maximum_fusion.2.source, f32[40,128]{1,0:T(8,128)S(1)} %bitcast.33), custom_call_target="tpu_custom_call" | custom-call | flops 4718592 | bytes 104857600 | tf_op jit(solution)/shard_map/pallas_call | solution.py:297
  (261 shorter events, 108.3 us)
Async XLA Ops:
  8.0 183.5 %all-gather.3.cloned.1.call-start = ((), (), s32[]{:S(2)}) async-start(), calls=%async_computation.2 | async-start | bytes 1769472 | tf_op jit(solution)/shard_map/all_gather | solution.py:469
  9.2 19.5 %collective-permute-start = (bf16[384,384]{1,0:T(8,128)(2,1)S(1)}, bf16[384,384]{1,0:T(8,128)(2,1)}, u32[]{:S(2)}, u32[]{:S(2)}) collective-permute-start(bf16[384,384]{1,0:T(8,128)(2,1)S(1)} %slice.104), channel_id=1, source_target_pairs={{0,2},{2,0},{1,3},{3,1},{4,6},{6,4},{5,7},{7,5},{8,10},{10,8},{9,1... | collective-permute-start | bytes 884744 | tf_op jit(solution)/shard_map/ppermute | solution.py:361
  14.1 16.7 %collective-permute-start.8 = (bf16[384,768]{1,0:T(8,128)(2,1)}, bf16[384,768]{1,0:T(8,128)(2,1)}, u32[]{:S(2)}, u32[]{:S(2)}) collective-permute-start(bf16[384,768]{1,0:T(8,128)(2,1)} %constant_dynamic-slice_fusion), channel_id=1, source_target_pairs={{0,1},{1,0},{2,3},{3,2},{4,5},{5,4},{6,7},{7,6},{8,9},{9,8},{10,11... | collective-permute-start | bytes 1769480 | tf_op jit(solution)/shard_map/ppermute | solution.py:377
  14.4 30.1 %collective-permute-start.7 = (bf16[960,384]{1,0:T(8,128)(2,1)S(1)}, bf16[960,384]{1,0:T(8,128)(2,1)S(1)}, u32[]{:S(2)}, u32[]{:S(2)}) collective-permute-start(bf16[960,384]{1,0:T(8,128)(2,1)S(1)} %pad_maximum_fusion.8), channel_id=1, source_target_pairs={{0,1},{1,3},{2,0},{3,2},{4,5},{5,7},{6,4},{7,6},{8,9},{9,11},{10,8... | collective-permute-start | bytes 2211848 | tf_op jit(solution)/shard_map/ppermute | solution.py:388
  15.9 28.6 %collective-permute-start.6 = (bf16[960,384]{1,0:T(8,128)(2,1)}, bf16[960,384]{1,0:T(8,128)(2,1)}, u32[]{:S(2)}, u32[]{:S(2)}) collective-permute-start(bf16[960,384]{1,0:T(8,128)(2,1)} %pad_maximum_fusion.7), channel_id=1, source_target_pairs={{0,0},{1,2},{2,1},{3,3},{4,4},{5,6},{6,5},{7,7},{8,8},{9,10},{10,9... | collective-permute-start | bytes 2211848 | tf_op jit(solution)/shard_map/ppermute | solution.py:387
  34.1 22.8 %collective-permute-start.4 = (bf16[384,384]{1,0:T(8,128)(2,1)S(1)}, bf16[384,384]{1,0:T(8,128)(2,1)S(1)}, u32[]{:S(2)}, u32[]{:S(2)}) collective-permute-start(bf16[384,384]{1,0:T(8,128)(2,1)S(1)} %slice.137.kv_ref), channel_id=1, source_target_pairs={{0,8},{4,12},{8,16},{12,20},{16,24},{20,28},{1,9},{5,13},{9,17},{1... | collective-permute-start | bytes 884744 | tf_op jit(solution)/shard_map/ppermute | solution.py:322
  37.8 19.1 %collective-permute-start.3 = (bf16[384,384]{1,0:T(8,128)(2,1)S(1)}, bf16[384,384]{1,0:T(8,128)(2,1)S(1)}, u32[]{:S(2)}, u32[]{:S(2)}) collective-permute-start(bf16[384,384]{1,0:T(8,128)(2,1)S(1)} %slice.137.kv_ref), channel_id=1, source_target_pairs={{0,12},{4,16},{8,20},{12,24},{16,28},{1,13},{5,17},{9,21},{13,25},... | collective-permute-start | bytes 884744 | tf_op jit(solution)/shard_map/ppermute | solution.py:322
  42.2 14.7 %collective-permute-start.2 = (bf16[384,384]{1,0:T(8,128)(2,1)S(1)}, bf16[384,384]{1,0:T(8,128)(2,1)S(1)}, u32[]{:S(2)}, u32[]{:S(2)}) collective-permute-start(bf16[384,384]{1,0:T(8,128)(2,1)S(1)} %slice.137.kv_ref), channel_id=1, source_target_pairs={{0,16},{4,20},{8,24},{12,28},{1,17},{5,21},{9,25},{13,29},{2,18},{... | collective-permute-start | bytes 884744 | tf_op jit(solution)/shard_map/ppermute | solution.py:322
  88.3 119.4 %reduce-scatter.7.cloned.1.call-start = ((), (), s32[]{:S(2)}) async-start(), calls=%async_computation.4 | async-start | bytes 737280
  90.7 35.4 %collective-permute-start.16 = (f32[3,384]{1,0:T(4,128)S(1)}, f32[3,384]{1,0:T(4,128)S(1)}, u32[]{:S(2)}, u32[]{:S(2)}) collective-permute-start(f32[3,384]{1,0:T(4,128)S(1)} %bitcast.43), channel_id=1, source_target_pairs={{16,0},{20,4},{24,8},{28,12},{17,1},{21,5},{25,9},{29,13},{18,2},{... | collective-permute-start | bytes 13832 | tf_op jit(solution)/shard_map/ppermute | solution.py:322
  92.2 32.7 %collective-permute-start.15 = (f32[3,384]{1,0:T(4,128)S(1)}, f32[3,384]{1,0:T(4,128)S(1)}, u32[]{:S(2)}, u32[]{:S(2)}) collective-permute-start(f32[3,384]{1,0:T(4,128)S(1)} %bitcast.44), channel_id=1, source_target_pairs={{12,0},{16,4},{20,8},{24,12},{28,16},{13,1},{17,5},{21,9},{25,13},... | collective-permute-start | bytes 13832 | tf_op jit(solution)/shard_map/ppermute | solution.py:322
  93.5 30.1 %collective-permute-start.14 = (f32[3,384]{1,0:T(4,128)S(1)}, f32[3,384]{1,0:T(4,128)S(1)}, u32[]{:S(2)}, u32[]{:S(2)}) collective-permute-start(f32[3,384]{1,0:T(4,128)S(1)} %bitcast.45), channel_id=1, source_target_pairs={{8,0},{12,4},{16,8},{20,12},{24,16},{28,20},{9,1},{13,5},{17,9},{2... | collective-permute-start | bytes 13832 | tf_op jit(solution)/shard_map/ppermute | solution.py:322
  94.8 27.0 %collective-permute-start.13 = (f32[3,384]{1,0:T(4,128)S(1)}, f32[3,384]{1,0:T(4,128)S(1)}, u32[]{:S(2)}, u32[]{:S(2)}) collective-permute-start(f32[3,384]{1,0:T(4,128)S(1)} %bitcast.46), channel_id=1, source_target_pairs={{4,0},{8,4},{12,8},{16,12},{20,16},{24,20},{28,24},{5,1},{9,5},{13... | collective-permute-start | bytes 13832 | tf_op jit(solution)/shard_map/ppermute | solution.py:322
  121.6 64.1 %collective-permute-start.18 = (bf16[384,960]{0,1:T(8,128)(2,1)}, bf16[384,960]{0,1:T(8,128)(2,1)S(1)}, u32[]{:S(2)}, u32[]{:S(2)}) collective-permute-start(bf16[384,960]{0,1:T(8,128)(2,1)} %copy.91), channel_id=1, source_target_pairs={{0,2},{1,0},{2,3},{3,1},{4,6},{5,4},{6,7},{7,5},{8,10},{9,8},{10,1... | collective-permute-start | bytes 2211848 | tf_op jit(solution)/shard_map/ppermute | solution.py:461
  121.7 196.1 %all-reduce.4.cloned.1.call-start = ((), (), s32[]{:S(2)}) async-start(), calls=%async_computation.5 | async-start | bytes 4718592 | tf_op jit(solution)/shard_map/psum | solution.py:474
  121.8 64.8 %collective-permute-start.17 = (bf16[384,960]{0,1:T(8,128)(2,1)}, bf16[384,960]{0,1:T(8,128)(2,1)S(1)}, u32[]{:S(2)}, u32[]{:S(2)}) collective-permute-start(bf16[384,960]{0,1:T(8,128)(2,1)} %copy.91), channel_id=1, source_target_pairs={{0,0},{1,2},{2,1},{3,3},{4,4},{5,6},{6,5},{7,7},{8,8},{9,10},{10,9... | collective-permute-start | bytes 2211848 | tf_op jit(solution)/shard_map/ppermute | solution.py:460
  124.8 21.2 %collective-permute-start.10 = (bf16[384,384]{1,0:T(8,128)(2,1)}, bf16[384,384]{1,0:T(8,128)(2,1)S(1)}, u32[]{:S(2)}, u32[]{:S(2)}) collective-permute-start(bf16[384,384]{1,0:T(8,128)(2,1)} %get-tuple-element.127), channel_id=1, source_target_pairs={{8,0},{12,4},{16,8},{20,12},{24,16},{28,20},{9,1},{13,5},{17,9},{2... | collective-permute-start | bytes 884744 | tf_op jit(solution)/shard_map/ppermute | solution.py:322
  126.2 34.3 %collective-permute-start.11 = (bf16[384,384]{1,0:T(8,128)(2,1)}, bf16[384,384]{1,0:T(8,128)(2,1)S(1)}, u32[]{:S(2)}, u32[]{:S(2)}) collective-permute-start(bf16[384,384]{1,0:T(8,128)(2,1)} %get-tuple-element.127), channel_id=1, source_target_pairs={{12,0},{16,4},{20,8},{24,12},{28,16},{13,1},{17,5},{21,9},{25,13},... | collective-permute-start | bytes 884744 | tf_op jit(solution)/shard_map/ppermute | solution.py:322
  135.9 49.8 %collective-permute-start.12 = (bf16[384,384]{1,0:T(8,128)(2,1)}, bf16[384,384]{1,0:T(8,128)(2,1)S(1)}, u32[]{:S(2)}, u32[]{:S(2)}) collective-permute-start(bf16[384,384]{1,0:T(8,128)(2,1)} %get-tuple-element.127), channel_id=1, source_target_pairs={{16,0},{20,4},{24,8},{28,12},{17,1},{21,5},{25,9},{29,13},{18,2},{... | collective-permute-start | bytes 884744 | tf_op jit(solution)/shard_map/ppermute | solution.py:322
  196.9 199.0 %reduce-scatter.5.cloned.1.call-start = ((), (), s32[]{:S(2)}) async-start(), calls=%async_computation.3 | async-start | bytes 983040 | tf_op jit(solution)/shard_map/reduce_scatter | solution.py:538
  202.3 34.2 %collective-permute-start.22 = (bf16[384,192]{1,0:T(8,128)(2,1)}, bf16[384,192]{1,0:T(8,128)(2,1)}, u32[]{:S(2)}, u32[]{:S(2)}) collective-permute-start(bf16[384,192]{1,0:T(8,128)(2,1)} %get-tuple-element.173.do_ref), channel_id=1, source_target_pairs={{16,0},{20,4},{24,8},{28,12},{17,1},{21,5},{25,9},{29,13},{18,2},{... | collective-permute-start | bytes 442376 | tf_op jit(solution)/shard_map/ppermute | solution.py:322
  203.5 32.0 %collective-permute-start.21 = (bf16[384,192]{1,0:T(8,128)(2,1)}, bf16[384,192]{1,0:T(8,128)(2,1)}, u32[]{:S(2)}, u32[]{:S(2)}) collective-permute-start(bf16[384,192]{1,0:T(8,128)(2,1)} %get-tuple-element.173.do_ref), channel_id=1, source_target_pairs={{12,0},{16,4},{20,8},{24,12},{28,16},{13,1},{17,5},{21,9},{25,13},... | collective-permute-start | bytes 442376 | tf_op jit(solution)/shard_map/ppermute | solution.py:322
  204.8 29.7 %collective-permute-start.20 = (bf16[384,192]{1,0:T(8,128)(2,1)}, bf16[384,192]{1,0:T(8,128)(2,1)}, u32[]{:S(2)}, u32[]{:S(2)}) collective-permute-start(bf16[384,192]{1,0:T(8,128)(2,1)} %get-tuple-element.173.do_ref), channel_id=1, source_target_pairs={{8,0},{12,4},{16,8},{20,12},{24,16},{28,20},{9,1},{13,5},{17,9},{2... | collective-permute-start | bytes 442376 | tf_op jit(solution)/shard_map/ppermute | solution.py:322
  206.1 22.8 %collective-permute-start.19 = (bf16[384,192]{1,0:T(8,128)(2,1)}, bf16[384,192]{1,0:T(8,128)(2,1)}, u32[]{:S(2)}, u32[]{:S(2)}) collective-permute-start(bf16[384,192]{1,0:T(8,128)(2,1)} %get-tuple-element.173.do_ref), channel_id=1, source_target_pairs={{4,0},{8,4},{12,8},{16,12},{20,16},{24,20},{28,24},{5,1},{9,5},{13... | collective-permute-start | bytes 442376 | tf_op jit(solution)/shard_map/ppermute | solution.py:322
  (45 other events, 432.3 us)
Sparse Core Ops, SparseCore 0:
  88.4 24.2 all-gather.2
  197.1 120.7 all-reduce.3
Sparse Core Ops, SparseCore 1:
  121.8 42.3 reduce-scatter.6
  324.4 22.0 reduce-scatter.4
